TPU v7x, 768 devices: a whole 4x8x12 slice. The times are simulated.
768 devices in a mesh: dp: 96 (over y, z), tensor: 8 (over x, core).
Axes of the slice: x: 4, y: 8, z: 12, core: 2. Of those that a mesh axis runs over, the one named last changes fastest.
Arguments:
- activations: bfloat16 [49152, 8192], P('dp', 'tensor'), may hold values from -6 to 6
- cotangent: bfloat16 [49152, 8192], P('dp', 'tensor'), may hold values from -0.0625 to 0.0625
- factor_down: float32 [8192, 64], P('tensor'), may hold values from -0.0625 to 0.0625
- factor_up: float32 [64, 8192], P(None, 'tensor'), may hold values from -0.75 to 0.75
- first_moment: float32 [8, 135168], P('tensor', 'dp'), may hold values from -4 to 4
- second_moment: float32 [8, 135168], P('tensor', 'dp'), may hold values from 0.01 to 1
- piece_lengths: int32 [8, 64], P('tensor'), may hold values from 1 to 4224, 135168 in all within a row
- writers: int32 [8, 64], P('tensor'), may hold values from 0 to 95
Outputs:
- partition: float32 [3, 8, 135168], P(None, 'tensor', 'dp')
- written: float32 [3, 96, 8, 135168], P(None, 'dp', 'tensor')
Inputs may be any that keep to these rules, and one draw needn't show every extreme that they name: `piece_lengths`: each row sums to 135168.
All inputs are finite; a program needn't handle non-finite values.
Results may differ from a plain program's by a relative error of at most 0.017.
Values may be sent and summed in bfloat16 or wider, within the bound.
No kernel may reach another device: no remote copies, remote signals or barrier semaphores. Data moves between devices by JAX's collectives and lax.ppermute only.
A program may use at most 64 MiB of HBM per device.

v0:
```python
import jax
import jax.numpy as jnp
from jax import lax
from jax.sharding import PartitionSpec as P


def flatten_local(left, right, total):
    pieces = [left.reshape(-1), right.reshape(-1)]
    used = left.size + right.size
    pieces.append(jnp.zeros((total - used,), jnp.float32))
    return jnp.concatenate(pieces)


def adam_update(param, grad, moment_one, moment_two):
    fresh_one = 0.9 * moment_one + 0.1 * grad
    fresh_two = 0.999 * moment_two + 0.001 * grad * grad
    fixed_one = 1.0 - 0.9**10
    fixed_two = 1.0 - 0.999**10
    updated = param - 0.01 * (fresh_one / fixed_one) / (jnp.sqrt(fresh_two / fixed_two) + 1e-08)
    return jnp.stack([updated, fresh_one, fresh_two])


def body(
    activations,
    cotangent,
    factor_down,
    factor_up,
    first_moment,
    second_moment,
    piece_lengths,
    writers,
):
    dp_count = lax.axis_size("dp")
    part_len = first_moment.shape[1]
    flat_len = part_len * dp_count
    my_rank = lax.axis_index("dp")
    down_b = factor_down.astype(jnp.bfloat16)
    up_b = factor_up.astype(jnp.bfloat16)
    reduced_part = jnp.dot(activations, down_b, preferred_element_type=jnp.float32).astype(
        jnp.bfloat16
    )
    projected_part = jnp.dot(cotangent, up_b.T, preferred_element_type=jnp.float32).astype(
        jnp.bfloat16
    )
    reduced, projected = (
        lax.psum(reduced_part, "tensor").astype(jnp.float32),
        lax.psum(projected_part, "tensor").astype(jnp.float32),
    )
    reduced_b = reduced.astype(jnp.bfloat16)
    projected_b = projected.astype(jnp.bfloat16)
    contract = (((0,), (0,)), ((), ()))
    grad_up = 2.0 * lax.dot_general(
        reduced_b, cotangent, contract, preferred_element_type=jnp.float32
    )
    grad_down = 2.0 * lax.dot_general(
        activations, projected_b, contract, preferred_element_type=jnp.float32
    )
    flat_grad = flatten_local(grad_down, grad_up, flat_len)
    flat_param = flatten_local(factor_down, factor_up, flat_len)
    owners = jnp.repeat(writers[0], piece_lengths[0], total_repeat_length=flat_len)
    mine = owners == my_rank
    grad_part = lax.psum_scatter(flat_grad, "dp", scatter_dimension=0, tiled=True)
    param_part = lax.dynamic_slice_in_dim(flat_param, my_rank * part_len, part_len, 0)
    stacked = adam_update(param_part, grad_part, first_moment[0], second_moment[0])
    empty = jnp.zeros((3, flat_len), jnp.float32)
    piece = lax.all_gather(stacked, "dp", axis=1, tiled=True)
    start = jnp.int32(0)
    count = piece.shape[1]
    flags = lax.dynamic_slice_in_dim(mine, start, count, 0)
    kept = jnp.where(flags[None, :], piece, jnp.float32(0.0))
    gathered = lax.dynamic_update_slice(empty, kept, (jnp.int32(0), start))
    written = gathered[:, None, None, :]
    partition = stacked[:, None, :]
    return (partition, written)


def solution(mesh):
    in_specs = (
        P("dp", "tensor"),
        P("dp", "tensor"),
        P("tensor", None),
        P(None, "tensor"),
        P("tensor", "dp"),
        P("tensor", "dp"),
        P("tensor", None),
        P("tensor", None),
    )
    out_specs = (P(None, "tensor", "dp"), P(None, "dp", "tensor", None))
    return jax.shard_map(body, mesh=mesh, in_specs=in_specs, out_specs=out_specs, check_vma=False)
```

profile of v0, /device:TPU:2, one launch (start us, length us, event | category | flops | bytes accessed | tf_op | source)
XLA Modules:
  0.0 465.8 jit_solution(12701803246845684556)
XLA Ops:
  7.2 0.0 copy-start
  7.2 0.0 copy-start.9
  7.2 0.0 copy-start.4
  7.2 0.0 all-reduce.9.cloned.1.call-start
  7.2 1.1 copy-done
  8.4 2.0 convolution_convert_fusion
  10.4 2.3 convolution_convert_fusion.1
  12.8 0.0 all-reduce.9.cloned.1.call-update
  12.8 0.0 all-reduce.7.cloned.1.call-start
  12.8 0.0 copy-done.9
  12.8 0.7 slice.40
  13.5 0.0 copy-done.4
  13.5 0.7 fusion.13
  14.2 0.7 fusion.16
  14.9 0.8 add_bitcast_fusion.1
  15.7 0.1 copy.21
  15.8 0.1 reduce-window.16
  15.9 0.1 fusion.7
  16.0 1.0 scatter_custom_fusion
  17.0 0.2 copy.22
  17.3 0.5 reduce-window.19
  17.9 0.3 reduce-window.24
  18.1 0.1 slice.180
  18.2 0.1 slice_reduce_fusion
  18.4 0.1 add_bitcast_fusion
  18.4 0.1 pad_slice_fusion
  18.5 0.1 add_add_fusion.1
  18.6 0.2 copy.24
  18.8 0.2 copy.23
  19.0 0.0 copy-start.1
  19.0 7.4 %compare_select_fusion.1 = (s32[135168,1]{0,1:T(1,128)}, s32[135168,1]{0,1:T(1,128)}) fusion(s32[]{:T(128)} %bitcast.68, s32[]{:T(128)} %bitcast.69, s32[]{:T(128)} %bitcast.70, s32[]{:T(128)} %bitcast.71, s32[]{:T(128)} %bitcast.72, s32[]{:T(128)} %bitcast.74, s32[]{:T(128)} %bitcast.73, s32[135168,1]{0,1:T(1,128)S(1)} %bitcast.100, ...), kind=kLoop, calls=%fused_computation.59 | loop fusion | flops 1892352 | bytes 2162716 | tf_op jit(solution)/shard_map/jit(_take)/gather | solution.py:60
  26.4 66.6 %all-reduce.9.cloned.1.call-done = (bf16[512,64]{0,1:T(8,128)(2,1)}, bf16[512,64]{0,1:T(8,128)(2,1)}) async-done(((bf16[512,64]{0,1:T(8,128)(2,1)}, bf16[512,64]{0,1:T(8,128)(2,1)}), (bf16[512,64]{0,1:T(8,128)(2,1)}, bf16[512,64]{0,1:T(8,128)(2,1)})) %all-reduce.9.cloned.1.call-update) | async-done | bytes 131088 | tf_op jit(solution)/shard_map/psum | solution.py:46
  93.0 1.9 fusion.1
  94.9 1.9 copy.20
  96.8 1.9 reshape.161
  98.7 0.0 copy-done.1
  98.7 0.0 copy-done.6
  98.7 0.3 fusion
  99.0 0.0 copy-start.3
  99.1 1.8 pad_maximum_fusion
  100.9 0.0 all-reduce.7.cloned.1.call-update
  100.9 0.0 all-gather.2.cloned.1.call-start
  101.0 0.0 copy-done.3
  101.0 110.5 %compare_reduce_fusion.56 = (pred[135168]{0:T(1024)(128)(4,1)S(1)}, pred[135168]{0:T(1024)(128)(4,1)}, pred[135168]{0:T(1024)(128)(4,1)}, pred[135168]{0:T(1024)...) fusion(s32[135168,1]{0,1:T(1,128)S(1)} %copy-done.3), kind=kLoop, calls=%fused_computation.58 | loop fusion | flops 7704576 | bytes 8245248 | tf_op jit(solution)/shard_map/jit(_take)/gather | solution.py:60
  211.5 1.2 copy.19
  212.7 0.8 reshape.159
  213.5 1.0 copy.27
  214.6 1.3 dynamic-slice.6
  216.5 0.7 fusion.15
  217.2 0.7 fusion.14
  217.9 0.0 copy-done.7
  218.0 0.0 copy-done.8
  218.0 112.7 %all-reduce.7.cloned.1.call-done = f32[135168]{0:T(1024)} async-done(((f32[135168]{0:T(1024)}), f32[135168]{0:T(1024)}) %all-reduce.7.cloned.1.call-update) | async-done | bytes 540688
  330.7 0.8 fusion.9
  331.5 0.6 pad_maximum_fusion.1
  332.2 0.0 all-gather.2.cloned.1.call-update
  332.2 0.0 copy-done.2
  332.2 0.0 copy-start.5
  332.2 42.2 %fusion.2 = pred[135168]{0:T(1024)(128)(4,1)S(1)} fusion(pred[135168]{0:T(1024)(128)(4,1)} %get-tuple-element.70, pred[135168]{0:T(1024)(128)(4,1)} %get-tuple-element.69, pred[135168]{0:T(1024)(128)(4,1)} %get-tuple-element.68, pred[135168]{0:T(1024)(128)(4,1)} %get-tuple-element.67, pred[135168]{0:T(1024)(128)(4,1)} %get-tuple-element.66, ...), kind=kLoop, calls=%fused_computation.78 | loop fusion | flops 8650752 | bytes 9461992 | tf_op jit(solution)/shard_map/eq | solution.py:61
  374.4 0.0 copy-done.5
  374.4 0.6 broadcast_in_dim.34
  375.0 79.8 %all-gather.2.cloned.1.call-done = f32[3,135168]{1,0:T(4,128)} async-done(((f32[3,1408]{1,0:T(4,128)}), f32[3,135168]{1,0:T(4,128)}) %all-gather.2.cloned.1.call-update) | async-done | bytes 1622032 | tf_op jit(solution)/shard_map/all_gather | solution.py:66
  454.9 2.0 broadcast_select_fusion
  456.9 2.4 broadcast_in_dim.41
  (16 shorter events, 0.2 us)
Async XLA Ops:
  7.2 1.2 copy-start
  7.2 5.7 %copy-start.9 = (s32[1,64]{1,0:T(1,128)S(1)}, s32[1,64]{1,0:T(1,128)}, u32[]{:S(2)}) copy-start(s32[1,64]{1,0:T(1,128)} %param.16) | copy-start | bytes 772
  7.2 6.3 %copy-start.4 = (s32[1,64]{1,0:T(1,128)S(1)}, s32[1,64]{1,0:T(1,128)}, u32[]{:S(2)}) copy-start(s32[1,64]{1,0:T(1,128)} %param.17) | copy-start | bytes 772
  7.2 85.8 %all-reduce.9.cloned.1.call-start = ((), (), s32[]{:S(2)}) async-start(), calls=%async_computation.2 | async-start | bytes 262144 | tf_op jit(solution)/shard_map/psum | solution.py:46
  12.8 317.9 %all-reduce.7.cloned.1.call-start = ((), (), s32[]{:S(2)}) async-start(), calls=%async_computation.1 | async-start | bytes 1081344
  19.0 79.7 %copy-start.1 = (bf16[512,1024]{1,0:T(8,128)(2,1)S(1)}, bf16[512,1024]{1,0:T(8,128)(2,1)}, u32[]{:S(2)}) copy-start(bf16[512,1024]{1,0:T(8,128)(2,1)} %param.11) | copy-start | bytes 3145732
  93.0 5.7 %copy-start.6 = (bf16[512,64]{0,1:T(8,128)(2,1)S(1)}, bf16[512,64]{0,1:T(8,128)(2,1)}, u32[]{:S(2)}) copy-start(bf16[512,64]{0,1:T(8,128)(2,1)} %get-tuple-element.71) | copy-start | bytes 196612
  99.0 2.0 copy-start.3
  100.9 353.9 %all-gather.2.cloned.1.call-start = ((), (), s32[]{:S(2)}) async-start(), calls=%async_computation | async-start | bytes 2185216 | tf_op jit(solution)/shard_map/all_gather | solution.py:66
  211.5 6.5 %copy-start.7 = (f32[1,1408]{1,0:T(1,128)S(1)}, f32[1,1408]{1,0:T(1,128)}, u32[]{:S(2)}) copy-start(f32[1,1408]{1,0:T(1,128)} %param.15) | copy-start | bytes 16900
  211.5 6.5 %copy-start.8 = (f32[1,1408]{1,0:T(1,128)S(1)}, f32[1,1408]{1,0:T(1,128)}, u32[]{:S(2)}) copy-start(f32[1,1408]{1,0:T(1,128)} %param.14) | copy-start | bytes 16900
  211.5 120.7 %copy-start.2 = (s32[135168,1]{0,1:T(1,128)S(1)}, s32[135168,1]{0,1:T(1,128)}, u32[]{:S(2)}) copy-start(s32[135168,1]{0,1:T(1,128)} %get-tuple-element.73) | copy-start | bytes 1622020
  332.2 42.2 %copy-start.5 = (f32[3,1408]{1,0:T(4,128)S(1)}, f32[3,1408]{1,0:T(4,128)}, u32[]{:S(2)}) copy-start(f32[3,1408]{1,0:T(4,128)} %pad_maximum_fusion.1) | copy-start | bytes 50692
Sparse Core Ops, SparseCore 0:
  12.9 80.0 all-reduce.8
  101.0 229.5 all-reduce.6
  335.0 119.7 all-gather.1
where the time goes:
time: 467 us; the launch traced here: 466 us
  waiting for transfers between devices  259 us (55%)
  other arithmetic  168 us (36%)
  local copies, waits for them, and re-layouts  16.9 us (4%)
  between operations  14.7 us (3%)
  matrix products  6.52 us (1%)
    gather x2, other arithmetic, body(): jnp.repeat(writers[0], piece_lengths[0], total_repeat_length=flat_len)  118 us
    unnamed x4, waiting for transfers between devices  113 us
    all_gather x1, waiting for transfers between devices, body(): piece = lax.all_gather(stacked, 'dp', axis=1, tiled=True)  79.8 us
    psum x1, waiting for transfers between devices, body(): lax.psum(reduced_part, 'tensor').astype(jnp.float32)  66.6 us
    eq x1, other arithmetic, body(): mine = owners == my_rank  42.2 us
  transfers between devices with their start and end apart: 3, of which 3 were waited for; matrix products, arithmetic and copies ran while one was open for 37% of the time, Pallas kernels for 0%

commit v1 on v0

v1 whole, which is shorter than its diff:
```python
import functools

import jax
import jax.numpy as jnp
from jax import lax
from jax.experimental import pallas as pl
from jax.experimental.pallas import tpu as pltpu
from jax.sharding import Mesh, PartitionSpec as P

BF16 = jnp.bfloat16
F32 = jnp.float32
LANES = 128
VMEM = pl.BlockSpec(memory_space=pltpu.VMEM)
HBM = pl.BlockSpec(memory_space=pltpu.HBM)
SMEM = pl.BlockSpec(memory_space=pltpu.SMEM)
NT = (((1,), (1,)), ((), ()))
PARAMS = pltpu.CompilerParams(vmem_limit_bytes=16 * 1024 * 1024)


def low_rank_kernel(rows, act, cot, down_t, up, first, second, out, packed, a, c, d, u, one, two, sems):
    count = sems.shape[0] // 2 - 2
    tall = act.shape[0] // count
    weights = [pltpu.make_async_copy(down_t, d, sems.at[0]), pltpu.make_async_copy(up, u, sems.at[1])]
    moments = [pltpu.make_async_copy(first, one, sems.at[2]), pltpu.make_async_copy(second, two, sems.at[3])]
    blocks = []
    for i in range(count):
        at = pl.ds(i * tall, tall)
        blocks.append(
            (
                pltpu.make_async_copy(act.at[at], a.at[at], sems.at[4 + 2 * i]),
                pltpu.make_async_copy(cot.at[at], c.at[at], sems.at[5 + 2 * i]),
            )
        )
    for copy in weights + [copy for pair in blocks for copy in pair] + moments:
        copy.start()
    for copy in weights:
        copy.wait()
    down_b = d[...].astype(BF16)
    up_b = u[...].astype(BF16)
    blank = jnp.zeros_like(down_b)
    left = jnp.concatenate([down_b, blank], axis=0)
    right = jnp.concatenate([blank, up_b], axis=0)
    for i, pair in enumerate(blocks):
        at = slice(i * tall, (i + 1) * tall)
        pair[0].wait()
        both = lax.dot_general(a[at], left, NT, preferred_element_type=F32)
        pair[1].wait()
        both += lax.dot_general(c[at], right, NT, preferred_element_type=F32)
        out[at, :] = both.astype(BF16)
    for copy in moments:
        copy.wait()
    half = packed.shape[0] // 2
    packed[...] = jnp.zeros_like(packed)
    for i, source in enumerate((one, two)):
        for r in range(rows):
            packed[half * i + r : half * i + r + 1, :] = source[:, r * LANES : (r + 1) * LANES]


def add_copies_kernel(mine, other, out):
    total = (mine[...].astype(F32) + other[...].astype(F32)).astype(BF16)
    for i in range(out.shape[0]):
        out[i] = total


def store_flat(flat, wide, down_t2, up):
    width = up.shape[1]
    rank = up.shape[0]
    half = width // 2
    per_row = width // LANES
    wide[...] = down_t2.T
    even = wide[pl.ds(0, half, stride=2), :]
    odd = wide[pl.ds(1, half, stride=2), :]
    lane = lax.broadcasted_iota(jnp.int32, (half, LANES), 1)
    flat[0:half, :] = jnp.where(lane < rank, even, odd)
    for c in range(per_row):
        flat[pl.ds(half + c, rank, stride=per_row), :] = up[:, c * LANES : (c + 1) * LANES]
    used = half + rank * per_row
    flat[used:, :] = jnp.zeros((flat.shape[0] - used, LANES), F32)


def param_kernel(down_t, up, flat, wide):
    left = down_t[...]
    store_flat(flat, wide, jnp.concatenate([left, left], axis=0), up[...])


def grad_kernel(rows, parts, act, cot, out, flat, wide):
    total = parts[0].astype(F32)
    for i in range(1, parts.shape[0]):
        total += parts[i].astype(F32)
    turned = total.T.astype(BF16)
    rank = turned.shape[0] // 2
    projected = turned[rank:]
    twice = jnp.concatenate([projected, projected], axis=0)
    up = 2.0 * jnp.dot(turned[:rank], cot[...], preferred_element_type=F32)
    down = 2.0 * jnp.dot(twice, act[...], preferred_element_type=F32)
    store_flat(flat, wide, down, up)
    part = out.shape[1]
    for j in range(out.shape[0]):
        for i in range(out.shape[2] // LANES):
            at = rows * j + part * i
            out[j, :, i * LANES : (i + 1) * LANES] = flat[at : at + part, :].astype(BF16)


def adam(param, grad, moment_one, moment_two):
    fresh_one = moment_one + 0.1 * grad
    fresh_two = moment_two + 0.001 * grad * grad
    fixed_one = 1.0 - 0.9**10
    fixed_two = 1.0 - 0.999**10
    updated = param - 0.01 * (fresh_one / fixed_one) / (jnp.sqrt(fresh_two / fixed_two) + 1e-08)
    return updated, fresh_one, fresh_two


def partition_kernel(rows, me, parts, flat, first, second, out, send, grad, one, two):
    total = jnp.sum(parts[...].astype(F32), axis=0)
    part = total.shape[0]
    for i in range(total.shape[1] // LANES):
        grad[part * i : part * (i + 1), :] = total[:, i * LANES : (i + 1) * LANES]
    packed = total.astype(BF16)
    for j in range(send.shape[0]):
        send[j] = packed
    for r in range(rows):
        one[r : r + 1, :] = first[:, r * LANES : (r + 1) * LANES]
        two[r : r + 1, :] = second[:, r * LANES : (r + 1) * LANES]
    param = flat[pl.ds(me[0] * rows, grad.shape[0]), :]
    fresh = adam(param, grad[...], 0.9 * one[...], 0.999 * two[...])
    for i in range(3):
        for r in range(rows):
            out[i, :, r * LANES : (r + 1) * LANES] = fresh[i][r : r + 1, :]


def prepare_kernel(rows, me, lengths, writers, packed, one, two, mask):
    mask[...] = jnp.zeros_like(mask)
    block = 8 * LANES
    spot = lax.broadcasted_iota(jnp.int32, (8, LANES), 0) * LANES + lax.broadcasted_iota(
        jnp.int32, (8, LANES), 1
    )

    def piece(k, start):
        end = start + lengths[0, k]

        @pl.when(writers[0, k] == me[0])
        def _():
            def mark(b, carry):
                here = spot + b * block
                at = pl.ds(pl.multiple_of(b * 8, 8), 8)
                inside = jnp.logical_and(here >= start, here < end)
                mask[at, :] = jnp.where(inside, 1.0, mask[at, :])
                return carry

            lax.fori_loop(start // block, (end + block - 1) // block, mark, 0)

        return end

    lax.fori_loop(0, lengths.shape[1], piece, 0)
    count = one.shape[0] // rows
    half = packed.shape[0] // count // 2
    for j in range(count):
        base = 2 * half * j
        tall = min(half, one.shape[0] - rows * j)
        one[rows * j : rows * j + tall, :] = 0.9 * packed[base : base + tall, :]
        two[rows * j : rows * j + tall, :] = 0.999 * packed[base + half : base + half + tall, :]


def written_kernel(rows, grads, first, second, flat, mask, out, grad, fresh, sems):
    part = grads.shape[1]
    steps = sems.shape[0]
    per_step = grads.shape[0] // steps
    tall = per_step * rows
    copies = []
    for s in range(steps):
        for j in range(s * per_step, (s + 1) * per_step):
            for i in range(grads.shape[2] // LANES):
                at = rows * j + part * i
                grad[at : at + part, :] = grads[j, :, i * LANES : (i + 1) * LANES].astype(F32)
        for r in range(s * tall, (s + 1) * tall, 24):
            at = slice(r, r + 24)
            keep = mask[at, :] > 0.0
            values = adam(flat[at, :], grad[at, :], first[at, :], second[at, :])
            for i in range(3):
                fresh[i, at, :] = jnp.where(keep, values[i], 0.0)
        block = pl.ds(s * tall, tall)
        copies.append(pltpu.make_async_copy(fresh.at[:, block], out.at[:, block], sems.at[s]))
        copies[-1].start()
    for copy in copies:
        copy.wait()


def gather_moments(packed, dp):
    return lax.all_gather(packed, dp, axis=0, tiled=True)


def body(dp, activations, cotangent, factor_down, factor_up, first_moment, second_moment, piece_lengths, writers):
    dp_count = lax.axis_size(dp)
    part_len = first_moment.shape[1]
    rows = part_len // LANES
    all_rows = rows * dp_count
    part = 4
    lanes = -(-rows // part) * LANES
    tokens, width = activations.shape
    rank = factor_up.shape[0]
    me = lax.axis_index(dp).astype(jnp.int32).reshape(1)
    down_t = factor_down.T
    x_count = lax.axis_size("x")

    blocks = 4
    partial, packed = pl.pallas_call(
        functools.partial(low_rank_kernel, rows),
        out_shape=(
            jax.ShapeDtypeStruct((tokens, 2 * rank), BF16),
            jax.ShapeDtypeStruct((24, LANES), F32),
        ),
        in_specs=[HBM] * 6,
        out_specs=(VMEM, VMEM),
        scratch_shapes=[
            pltpu.VMEM((tokens, width), BF16),
            pltpu.VMEM((tokens, width), BF16),
            pltpu.VMEM((rank, width), F32),
            pltpu.VMEM((rank, width), F32),
            pltpu.VMEM((1, part_len), F32),
            pltpu.VMEM((1, part_len), F32),
            pltpu.SemaphoreType.DMA((4 + 2 * blocks,)),
        ],
        compiler_params=pltpu.CompilerParams(vmem_limit_bytes=56 * 1024 * 1024),
        name="low_rank",
    )(activations, cotangent, down_t, factor_up, first_moment, second_moment)
    all_moments = gather_moments(packed, dp)
    other = lax.ppermute(partial, "c", [(0, 1), (1, 0)])
    flat_param = pl.pallas_call(
        param_kernel,
        out_shape=jax.ShapeDtypeStruct((all_rows + 8, LANES), F32),
        in_specs=[VMEM] * 2,
        out_specs=VMEM,
        scratch_shapes=[pltpu.VMEM((width, LANES), F32)],
        compiler_params=PARAMS,
        name="flat_param",
    )(down_t, factor_up)
    copies = pl.pallas_call(
        add_copies_kernel,
        out_shape=jax.ShapeDtypeStruct((x_count, tokens, 2 * rank), BF16),
        in_specs=[VMEM] * 2,
        out_specs=VMEM,
        compiler_params=PARAMS,
        name="add_cores",
    )(partial, other)
    parts = lax.all_to_all(copies, "x", 0, 0)
    chunks = pl.pallas_call(
        functools.partial(grad_kernel, rows),
        out_shape=jax.ShapeDtypeStruct((dp_count, part, lanes), BF16),
        in_specs=[VMEM] * 3,
        out_specs=VMEM,
        scratch_shapes=[
            pltpu.VMEM((all_rows + 8, LANES), F32),
            pltpu.VMEM((width, LANES), F32),
        ],
        compiler_params=PARAMS,
        name="grads",
    )(parts, activations, cotangent)
    mine = lax.all_to_all(chunks, dp, 0, 0)
    partition, send = pl.pallas_call(
        functools.partial(partition_kernel, rows),
        out_shape=(
            jax.ShapeDtypeStruct((3, 1, part_len), F32),
            jax.ShapeDtypeStruct((dp_count, part, lanes), BF16),
        ),
        in_specs=[SMEM] + [VMEM] * 4,
        out_specs=(VMEM, VMEM),
        scratch_shapes=[pltpu.VMEM((lanes * part // LANES, LANES), F32)] * 3,
        compiler_params=PARAMS,
        name="partition",
    )(me, mine, flat_param, first_moment, second_moment)
    grads = lax.all_to_all(send, dp, 0, 0)
    one, two, mask = pl.pallas_call(
        functools.partial(prepare_kernel, rows),
        out_shape=[jax.ShapeDtypeStruct((all_rows, LANES), F32)] * 3,
        in_specs=[SMEM] * 3 + [VMEM],
        out_specs=[VMEM] * 3,
        compiler_params=PARAMS,
        name="prepare",
    )(me, piece_lengths, writers, all_moments)
    written = pl.pallas_call(
        functools.partial(written_kernel, rows),
        out_shape=jax.ShapeDtypeStruct((3, all_rows, LANES), F32),
        in_specs=[VMEM] * 5,
        out_specs=HBM,
        scratch_shapes=[
            pltpu.VMEM((all_rows + 8, LANES), F32),
            pltpu.VMEM((3, all_rows, LANES), F32),
            pltpu.SemaphoreType.DMA((4,)),
        ],
        compiler_params=PARAMS,
        name="written",
    )(grads, one, two, flat_param, mask)
    return (partition, written.reshape(3, 1, 1, all_rows * LANES))


def solution(mesh):
    fine = Mesh(mesh.devices.reshape(8, 12, 4, 2), ("y", "z", "x", "c"))
    return on_mesh(fine)


def on_mesh(fine):
    dp, tensor = ("y", "z"), ("x", "c")
    in_specs = (
        P(dp, tensor),
        P(dp, tensor),
        P(tensor, None),
        P(None, tensor),
        P(tensor, dp),
        P(tensor, dp),
        P(tensor, None),
        P(tensor, None),
    )
    out_specs = (P(None, tensor, dp), P(None, dp, tensor, None))
    return jax.shard_map(
        functools.partial(body, dp), mesh=fine, in_specs=in_specs, out_specs=out_specs, check_vma=False
    )
```

time: 467 us -> 152 us (0.33)
  waiting for transfers between devices: 259 us -> 83 us
  other arithmetic: 168 us -> 0 us
  starting transfers between devices: 0.12 us -> 22.6 us
  blocking collectives: 0 us -> 20.6 us
  local copies, waits for them, and re-layouts: 16.9 us -> 2.21 us
  Pallas kernels: 0 us -> 9.45 us
  matrix products: 6.52 us -> 0 us
    gather x2 -> x0, other arithmetic: 118 us -> none  [body(): jnp.repeat(writers[0], piece_lengths[0], total_repeat_length=flat_len)]
    unnamed x4 -> x1, waiting for transfers between devices: 113 us -> 0.02 us
    psum x1 -> x0, waiting for transfers between devices: 66.6 us -> none  [body(): lax.psum(reduced_part, 'tensor').astype(jnp.float32)]
    eq x1 -> x0, other arithmetic: 42.2 us -> none  [body(): mine = owners == my_rank]
    all_to_all x0 -> x2, starting transfers between devices: none -> 20.7 us  [the longest x1 14.5 us: body(): mine = lax.all_to_all(chunks, dp, 0, 0)]
    all_to_all x0 -> x1, blocking collectives: none -> 20.6 us  [body(): parts = lax.all_to_all(copies, 'x', 0, 0)]
    all_to_all x0 -> x2, waiting for transfers between devices: none -> 18.6 us  [the longest x1 18.6 us: body(): mine = lax.all_to_all(chunks, dp, 0, 0)]
    all_gather x1, waiting for transfers between devices: 79.8 us -> 62.9 us  [gather_moments(): return lax.all_gather(packed, dp, axis=0, tiled=True)]
  transfers between devices with their start and end apart: 3 -> 4, of which waited for: 3 -> 3; matrix products, arithmetic and copies ran while one was open for 37% -> 0% of each run, Pallas kernels for 0% -> 3%
where the time goes in v1:
time: 152 us
  waiting for transfers between devices  83 us (55%)
  starting transfers between devices  22.6 us (15%)
  blocking collectives  20.6 us (14%)
  between operations  14.2 us (9%)
  Pallas kernels  9.45 us (6%)
  local copies, waits for them, and re-layouts  2.21 us (1%)
    all_gather x1, waiting for transfers between devices, gather_moments(): return lax.all_gather(packed, dp, axis=0, tiled=True)  62.9 us
    all_to_all x1, blocking collectives, body(): parts = lax.all_to_all(copies, 'x', 0, 0)  20.6 us
    all_to_all x1, waiting for transfers between devices, body(): mine = lax.all_to_all(chunks, dp, 0, 0)  18.6 us
    all_to_all x1, starting transfers between devices, body(): mine = lax.all_to_all(chunks, dp, 0, 0)  14.5 us
    all_to_all x1, starting transfers between devices, body(): grads = lax.all_to_all(send, dp, 0, 0)  6.12 us
    pallas_call x1, Pallas kernels, body(): pl.pallas_call(functools.partial(low_rank_kernel, rows), out_shape=(jax.S...  3.82 us
  transfers between devices with their start and end apart: 4, of which 3 were waited for; matrix products, arithmetic and copies ran while one was open for 0% of the time, Pallas kernels for 3%

profile of v1, /device:TPU:2, one launch (start us, length us, event | category | flops | bytes accessed | tf_op | source)
XLA Modules:
  0.0 152.0 jit_solution(3266572239465233444)
XLA Ops:
  7.2 0.0 all-gather.2.cloned.1.call-start
  7.2 0.0 copy-start
  7.2 0.0 copy-start.1
  7.2 3.8 %low_rank.1 = (bf16[512,128]{1,0:T(8,128)(2,1)}, f32[24,128]{1,0:T(8,128)}) custom-call(bf16[512,1024]{1,0:T(8,128)(2,1)} %act.3, bf16[512,1024]{1,0:T(8,128)(2,1)} %cot.3, f32[64,1024]{1,0:T(8,128)} %bitcast.3, f32[64,1024]{1,0:T(8,128)} %up.3, f32[1,1408]{1,0:T(1,128)} %first.3, f32[1,1408]{1,0:T(1,128)} %second.3), custom_call_target="tpu_custom_call" | custom-call | tf_op jit(solution)/shard_map/low_rank/pallas_call | solution.py:206
  11.1 0.0 all-gather.2.cloned.1.call-update
  11.1 1.9 %collective-permute-start = (bf16[512,128]{1,0:T(8,128)(2,1)}, bf16[512,128]{1,0:T(8,128)(2,1)S(1)}, u32[]{:S(2)}, u32[]{:S(2)}) collective-permute-start(bf16[512,128]{1,0:T(8,128)(2,1)} %get-tuple-element.9.mine), channel_id=1, source_target_pairs={{0,1},{1,0},{2,3},{3,2},{4,5},{5,4},{6,7},{7,6},{8,9},{9,8},{10,11... | collective-permute-start | bytes 393224 | tf_op jit(solution)/shard_map/ppermute | solution.py:227
  13.0 1.5 %collective-permute-done.other = bf16[512,128]{1,0:T(8,128)(2,1)S(1)} collective-permute-done((bf16[512,128]{1,0:T(8,128)(2,1)}, bf16[512,128]{1,0:T(8,128)(2,1)S(1)}, u32[]{:S(2)}, u32[]{:S(2)}) %collective-permute-start) | collective-permute-done | bytes 131104 | tf_op jit(solution)/shard_map/ppermute | solution.py:227
  14.5 0.0 copy-start.5
  14.5 0.9 copy-done.5
  15.5 20.6 %all_to_all.15.parts = bf16[4,512,128]{2,1,0:T(8,128)(2,1)S(1)} all-to-all(bf16[4,512,128]{2,1,0:T(8,128)(2,1)S(1)} %add_cores.1), channel_id=1, replica_groups=mesh['y'=8,'z'=12,'x'=4,'c'=2] {'x'}, dimensions={0} | all-to-all | bytes 1048576 | tf_op jit(solution)/shard_map/all_to_all | solution.py:245
  36.0 0.0 copy-done
  36.0 0.0 copy-done.1
  36.0 0.0 copy-start.3
  36.0 0.0 copy-start.4
  36.1 0.0 copy-start.6
  36.1 0.0 copy-start.7
  36.1 1.5 grads.1
  37.5 0.0 copy-start.8
  37.5 0.0 copy-start.9
  37.5 14.5 %all-to-all-start.1 = ((bf16[96,4,384]{2,1,0:T(4,128)(2,1)}), bf16[96,4,384]{2,1,0:T(4,128)(2,1)S(1)}, u32[]{:S(2)}, u32[]{:S(2)}) async-start(bf16[96,4,384]{2,1,0:T(4,128)(2,1)} %grads.1), calls=%async_computation.1 | async-start | bytes 589824 | tf_op jit(solution)/shard_map/all_to_all | solution.py:258
  52.1 0.0 copy-done.3
  52.1 0.0 copy-done.4
  52.1 0.2 flat_param.1.flat
  52.4 18.6 %all-to-all-done.1.parts = bf16[96,4,384]{2,1,0:T(4,128)(2,1)S(1)} async-done(((bf16[96,4,384]{2,1,0:T(4,128)(2,1)}), bf16[96,4,384]{2,1,0:T(4,128)(2,1)S(1)}, u32[]{:S(2)}, u32[]{:S(2)}) %all-to-all-start.1) | async-done | bytes 294944 | tf_op jit(solution)/shard_map/all_to_all | solution.py:258
  71.0 0.0 copy-done.6
  71.0 0.0 copy-done.7
  71.0 0.9 partition.1
  71.8 6.1 %all-to-all-start.2 = ((bf16[96,4,384]{2,1,0:T(4,128)(2,1)}), bf16[96,4,384]{2,1,0:T(4,128)(2,1)S(1)}, u32[]{:S(2)}, u32[]{:S(2)}) async-start(bf16[96,4,384]{2,1,0:T(4,128)(2,1)} %get-tuple-element.11), calls=%async_computation.2 | async-start | bytes 589824 | tf_op jit(solution)/shard_map/all_to_all | solution.py:271
  78.0 62.9 %all-gather.2.cloned.1.call-done.packed = f32[2304,128]{1,0:T(8,128)} async-done(((f32[24,128]{1,0:T(8,128)}), f32[2304,128]{1,0:T(8,128)}) %all-gather.2.cloned.1.call-update) | async-done | bytes 1179664 | tf_op jit(solution)/shard_map/all_gather | solution.py:189
  140.8 0.0 copy-done.8
  140.8 0.0 copy-done.9
  140.8 0.0 copy-start.2
  140.8 1.3 copy-done.2
  142.1 1.7 %prepare.1 = (f32[1056,128]{1,0:T(8,128)S(1)}, f32[1056,128]{1,0:T(8,128)S(1)}, f32[1056,128]{1,0:T(8,128)S(1)}) custom-call(s32[1]{0:T(128)} %bitcast.me, s32[1,64]{1,0:T(1,128)S(1)} %copy-done.8, s32[1,64]{1,0:T(1,128)S(1)} %copy-done.9, f32[2304,128]{1,0:T(8,128)S(1)} %copy-done.2), custom_call_target="tpu_custom_call" | custom-call | tf_op jit(solution)/shard_map/prepare/pallas_call | solution.py:272
  143.8 0.0 all-to-all-done.2.grads
  143.8 1.3 written.1
  (1 shorter events, 0.0 us)
Async XLA Ops:
  7.2 133.7 %all-gather.2.cloned.1.call-start = ((), (), s32[]{:S(2)}) async-start(), calls=%async_computation.3 | async-start | bytes 1191936 | tf_op jit(solution)/shard_map/all_gather | solution.py:189
  7.2 28.8 %copy-start = (bf16[512,1024]{1,0:T(8,128)(2,1)S(1)}, bf16[512,1024]{1,0:T(8,128)(2,1)}, u32[]{:S(2)}) copy-start(bf16[512,1024]{1,0:T(8,128)(2,1)} %act.3) | copy-start | bytes 3145732
  7.2 28.8 %copy-start.1 = (bf16[512,1024]{1,0:T(8,128)(2,1)S(1)}, bf16[512,1024]{1,0:T(8,128)(2,1)}, u32[]{:S(2)}) copy-start(bf16[512,1024]{1,0:T(8,128)(2,1)} %cot.3) | copy-start | bytes 3145732
  11.1 3.5 %collective-permute-start = (bf16[512,128]{1,0:T(8,128)(2,1)}, bf16[512,128]{1,0:T(8,128)(2,1)S(1)}, u32[]{:S(2)}, u32[]{:S(2)}) collective-permute-start(bf16[512,128]{1,0:T(8,128)(2,1)} %get-tuple-element.9.mine), channel_id=1, source_target_pairs={{0,1},{1,0},{2,3},{3,2},{4,5},{5,4},{6,7},{7,6},{8,9},{9,8},{10,11... | collective-permute-start | bytes 393224 | tf_op jit(solution)/shard_map/ppermute | solution.py:227
  14.5 0.9 copy-start.5
  36.0 16.0 %copy-start.3 = (f32[1024,64]{0,1:T(8,128)S(1)}, f32[1024,64]{0,1:T(8,128)}, u32[]{:S(2)}) copy-start(f32[1024,64]{0,1:T(8,128)} %param.10) | copy-start | bytes 786436
  36.0 16.1 %copy-start.4 = (f32[64,1024]{1,0:T(8,128)S(1)}, f32[64,1024]{1,0:T(8,128)}, u32[]{:S(2)}) copy-start(f32[64,1024]{1,0:T(8,128)} %up.3) | copy-start | bytes 786436
  36.1 34.9 %copy-start.6 = (f32[1,1408]{1,0:T(1,128)S(1)}, f32[1,1408]{1,0:T(1,128)}, u32[]{:S(2)}) copy-start(f32[1,1408]{1,0:T(1,128)} %first.3) | copy-start | bytes 16900
  36.1 34.9 %copy-start.7 = (f32[1,1408]{1,0:T(1,128)S(1)}, f32[1,1408]{1,0:T(1,128)}, u32[]{:S(2)}) copy-start(f32[1,1408]{1,0:T(1,128)} %second.3) | copy-start | bytes 16900
  37.5 103.3 %copy-start.8 = (s32[1,64]{1,0:T(1,128)S(1)}, s32[1,64]{1,0:T(1,128)}, u32[]{:S(2)}) copy-start(s32[1,64]{1,0:T(1,128)} %lengths.1) | copy-start | bytes 772
  37.5 103.3 %copy-start.9 = (s32[1,64]{1,0:T(1,128)S(1)}, s32[1,64]{1,0:T(1,128)}, u32[]{:S(2)}) copy-start(s32[1,64]{1,0:T(1,128)} %writers.1) | copy-start | bytes 772
  37.5 33.4 %all-to-all-start.1 = ((bf16[96,4,384]{2,1,0:T(4,128)(2,1)}), bf16[96,4,384]{2,1,0:T(4,128)(2,1)S(1)}, u32[]{:S(2)}, u32[]{:S(2)}) async-start(bf16[96,4,384]{2,1,0:T(4,128)(2,1)} %grads.1), calls=%async_computation.1 | async-start | bytes 589824 | tf_op jit(solution)/shard_map/all_to_all | solution.py:258
  71.8 72.0 %all-to-all-start.2 = ((bf16[96,4,384]{2,1,0:T(4,128)(2,1)}), bf16[96,4,384]{2,1,0:T(4,128)(2,1)S(1)}, u32[]{:S(2)}, u32[]{:S(2)}) async-start(bf16[96,4,384]{2,1,0:T(4,128)(2,1)} %get-tuple-element.11), calls=%async_computation.2 | async-start | bytes 589824 | tf_op jit(solution)/shard_map/all_to_all | solution.py:271
  140.8 1.3 copy-start.2
Sparse Core Ops, SparseCore 0:
  11.7 129.0 all-gather.1

commit v2 on v1

v2 whole, which is shorter than its diff:
```python
import functools

import jax
import jax.numpy as jnp
from jax import lax
from jax.experimental import pallas as pl
from jax.experimental.pallas import tpu as pltpu
from jax.sharding import Mesh, PartitionSpec as P

BF16 = jnp.bfloat16
F32 = jnp.float32
LANES = 128
VMEM = pl.BlockSpec(memory_space=pltpu.VMEM)
HBM = pl.BlockSpec(memory_space=pltpu.HBM)
SMEM = pl.BlockSpec(memory_space=pltpu.SMEM)
NT = (((1,), (1,)), ((), ()))
PARAMS = pltpu.CompilerParams(vmem_limit_bytes=16 * 1024 * 1024)


def low_rank_kernel(act, cot, down_t, up, out, a, c, d, u, sems):
    copies = [
        pltpu.make_async_copy(source, target, sems.at[i])
        for i, (source, target) in enumerate(((down_t, d), (act, a), (up, u), (cot, c)))
    ]
    for copy in copies:
        copy.start()
    copies[0].wait()
    down_b = d[...].astype(BF16)
    blank = jnp.zeros_like(down_b)
    left = jnp.concatenate([down_b, blank], axis=0)
    copies[1].wait()
    both = lax.dot_general(a[...], left, NT, preferred_element_type=F32)
    copies[2].wait()
    right = jnp.concatenate([blank, u[...].astype(BF16)], axis=0)
    copies[3].wait()
    both += lax.dot_general(c[...], right, NT, preferred_element_type=F32)
    out[...] = both.astype(BF16)


def add_copies_kernel(mine, other, out):
    total = (mine[...].astype(F32) + other[...].astype(F32)).astype(BF16)
    for i in range(out.shape[0]):
        out[i] = total


def store_flat(flat, wide, down_t2, up):
    width = up.shape[1]
    rank = up.shape[0]
    half = width // 2
    per_row = width // LANES
    wide[...] = down_t2.T
    even = wide[pl.ds(0, half, stride=2), :]
    odd = wide[pl.ds(1, half, stride=2), :]
    lane = lax.broadcasted_iota(jnp.int32, (half, LANES), 1)
    flat[0:half, :] = jnp.where(lane < rank, even, odd)
    for c in range(per_row):
        flat[pl.ds(half + c, rank, stride=per_row), :] = up[:, c * LANES : (c + 1) * LANES]
    used = half + rank * per_row
    flat[used:, :] = jnp.zeros((flat.shape[0] - used, LANES), F32)


def param_kernel(me, lengths, writers, down_t, up, flat, mask, wide):
    left = down_t[...]
    store_flat(flat, wide, jnp.concatenate([left, left], axis=0), up[...])
    mask[...] = jnp.zeros_like(mask)
    block = 8 * LANES
    spot = lax.broadcasted_iota(jnp.int32, (8, LANES), 0) * LANES + lax.broadcasted_iota(
        jnp.int32, (8, LANES), 1
    )

    def piece(k, start):
        end = start + lengths[0, k]

        @pl.when(writers[0, k] == me[0])
        def _():
            def mark(b, carry):
                here = spot + b * block
                at = pl.ds(pl.multiple_of(b * 8, 8), 8)
                inside = jnp.logical_and(here >= start, here < end)
                mask[at, :] = jnp.where(inside, 1.0, mask[at, :])
                return carry

            lax.fori_loop(start // block, (end + block - 1) // block, mark, 0)

        return end

    lax.fori_loop(0, lengths.shape[1], piece, 0)


def grad_kernel(rows, parts, act, cot, out, flat, wide):
    total = parts[0].astype(F32)
    for i in range(1, parts.shape[0]):
        total += parts[i].astype(F32)
    turned = total.T.astype(BF16)
    rank = turned.shape[0] // 2
    projected = turned[rank:]
    twice = jnp.concatenate([projected, projected], axis=0)
    up = 2.0 * jnp.dot(turned[:rank], cot[...], preferred_element_type=F32)
    down = 2.0 * jnp.dot(twice, act[...], preferred_element_type=F32)
    store_flat(flat, wide, down, up)
    part = out.shape[1]
    for j in range(out.shape[0]):
        for i in range(out.shape[2] // LANES):
            at = rows * j + part * i
            out[j, :, i * LANES : (i + 1) * LANES] = flat[at : at + part, :].astype(BF16)


def adam_moments(grad, moment_one, moment_two):
    return 0.9 * moment_one + 0.1 * grad, 0.999 * moment_two + 0.001 * grad * grad


def adam_param(param, fresh_one, fresh_two):
    fixed_one = 1.0 - 0.9**10
    fixed_two = 1.0 - 0.999**10
    return param - 0.01 * (fresh_one / fixed_one) / (jnp.sqrt(fresh_two / fixed_two) + 1e-08)


def partition_kernel(rows, me, parts, flat, first, second, out, send, grad, one, two):
    total = jnp.sum(parts[...].astype(F32), axis=0)
    part = total.shape[0]
    half = grad.shape[0]
    for i in range(total.shape[1] // LANES):
        grad[part * i : part * (i + 1), :] = total[:, i * LANES : (i + 1) * LANES]
    for r in range(rows):
        one[r : r + 1, :] = first[:, r * LANES : (r + 1) * LANES]
        two[r : r + 1, :] = second[:, r * LANES : (r + 1) * LANES]
    blank = jnp.zeros((half - rows, LANES), F32)
    one[rows:, :] = blank
    two[rows:, :] = blank
    fresh = adam_moments(grad[...], one[...], two[...])
    both = jnp.concatenate(fresh, axis=0).astype(BF16)
    for j in range(send.shape[0]):
        send[j] = both
    updated = adam_param(flat[pl.ds(me[0] * rows, half), :], *fresh)
    for i, values in enumerate((updated,) + fresh):
        for r in range(rows):
            out[i, :, r * LANES : (r + 1) * LANES] = values[r : r + 1, :]


def copies_kernel(source, out):
    values = source[...]
    for i in range(out.shape[0]):
        out[i] = values


def written_kernel(rows, moments, flat, mask, out, one, two, fresh, sems):
    half = moments.shape[1] // 2
    steps = sems.shape[0]
    per_step = moments.shape[0] // steps
    tall = per_step * rows
    copies = []
    for s in range(steps):
        for j in range(s * per_step, (s + 1) * per_step):
            values = moments[j].astype(F32)
            one[rows * j : rows * j + half, :] = values[:half]
            two[rows * j : rows * j + half, :] = values[half:]
        for r in range(s * tall, (s + 1) * tall, 24):
            at = slice(r, r + 24)
            keep = mask[at, :] > 0.0
            fresh_one, fresh_two = one[at, :], two[at, :]
            updated = adam_param(flat[at, :], fresh_one, fresh_two)
            for i, values in enumerate((updated, fresh_one, fresh_two)):
                fresh[i, at, :] = jnp.where(keep, values, 0.0)
        block = pl.ds(s * tall, tall)
        copies.append(pltpu.make_async_copy(fresh.at[:, block], out.at[:, block], sems.at[s]))
        copies[-1].start()
    for copy in copies:
        copy.wait()


def body(dp, activations, cotangent, factor_down, factor_up, first_moment, second_moment, piece_lengths, writers):
    dp_count = lax.axis_size(dp)
    part_len = first_moment.shape[1]
    rows = part_len // LANES
    all_rows = rows * dp_count
    part = 4
    lanes = -(-rows // part) * LANES
    tokens, width = activations.shape
    rank = factor_up.shape[0]
    me = lax.axis_index(dp).astype(jnp.int32).reshape(1)
    down_t = factor_down.T
    x_count = lax.axis_size("x")

    partial, act_copy, cot_copy = pl.pallas_call(
        low_rank_kernel,
        out_shape=(
            jax.ShapeDtypeStruct((tokens, 2 * rank), BF16),
            jax.ShapeDtypeStruct((tokens, width), BF16),
            jax.ShapeDtypeStruct((tokens, width), BF16),
        ),
        in_specs=[HBM] * 4,
        out_specs=(VMEM, VMEM, VMEM),
        scratch_shapes=[
            pltpu.VMEM((rank, width), F32),
            pltpu.VMEM((rank, width), F32),
            pltpu.SemaphoreType.DMA((4,)),
        ],
        compiler_params=PARAMS,
        name="low_rank",
    )(*[pltpu.with_memory_space_constraint(v, pltpu.HBM) for v in (activations, cotangent, down_t, factor_up)])
    other = lax.ppermute(partial, "c", [(0, 1), (1, 0)])
    flat_param, mask = pl.pallas_call(
        param_kernel,
        out_shape=(
            jax.ShapeDtypeStruct((all_rows + 8, LANES), F32),
            jax.ShapeDtypeStruct((all_rows, LANES), F32),
        ),
        in_specs=[SMEM] * 3 + [VMEM] * 2,
        out_specs=(VMEM, VMEM),
        scratch_shapes=[pltpu.VMEM((width, LANES), F32)],
        compiler_params=PARAMS,
        name="flat_param",
    )(me, piece_lengths, writers, down_t, factor_up)
    copies = pl.pallas_call(
        add_copies_kernel,
        out_shape=jax.ShapeDtypeStruct((x_count, tokens, 2 * rank), BF16),
        in_specs=[VMEM] * 2,
        out_specs=VMEM,
        compiler_params=PARAMS,
        name="add_cores",
    )(partial, other)
    parts = lax.all_to_all(copies, "x", 0, 0)
    chunks = pl.pallas_call(
        functools.partial(grad_kernel, rows),
        out_shape=jax.ShapeDtypeStruct((dp_count, part, lanes), BF16),
        in_specs=[VMEM] * 3,
        out_specs=VMEM,
        scratch_shapes=[
            pltpu.VMEM((all_rows + 8, LANES), F32),
            pltpu.VMEM((width, LANES), F32),
        ],
        compiler_params=PARAMS,
        name="grads",
    )(parts, act_copy, cot_copy)
    mine = lax.all_to_all(chunks, dp, 0, 0)
    half = lanes * part // LANES
    z_count = lax.axis_size(dp[1])
    partition, send = pl.pallas_call(
        functools.partial(partition_kernel, rows),
        out_shape=(
            jax.ShapeDtypeStruct((3, 1, part_len), F32),
            jax.ShapeDtypeStruct((z_count, 2 * half, LANES), BF16),
        ),
        in_specs=[SMEM] + [VMEM] * 4,
        out_specs=(VMEM, VMEM),
        scratch_shapes=[pltpu.VMEM((half, LANES), F32)] * 3,
        compiler_params=PARAMS,
        name="partition",
    )(me, mine, flat_param, first_moment, second_moment)
    row = lax.all_to_all(send, dp[1], 0, 0)
    row_copies = pl.pallas_call(
        copies_kernel,
        out_shape=jax.ShapeDtypeStruct((lax.axis_size(dp[0]), z_count * 2 * half, LANES), BF16),
        in_specs=[VMEM],
        out_specs=VMEM,
        compiler_params=PARAMS,
        name="row_copies",
    )(row.reshape(z_count * 2 * half, LANES))
    moments = lax.all_to_all(row_copies, dp[0], 0, 0)
    written = pl.pallas_call(
        functools.partial(written_kernel, rows),
        out_shape=jax.ShapeDtypeStruct((3, all_rows, LANES), F32),
        in_specs=[VMEM] * 3,
        out_specs=HBM,
        scratch_shapes=[
            pltpu.VMEM((all_rows + 8, LANES), F32),
            pltpu.VMEM((all_rows + 8, LANES), F32),
            pltpu.VMEM((3, all_rows, LANES), F32),
            pltpu.SemaphoreType.DMA((4,)),
        ],
        compiler_params=PARAMS,
        name="written",
    )(moments.reshape(dp_count, 2 * half, LANES), flat_param, mask)
    return (partition, written.reshape(3, 1, 1, all_rows * LANES))


def solution(mesh):
    fine = Mesh(mesh.devices.reshape(8, 12, 4, 2), ("y", "z", "x", "c"))
    return on_mesh(fine)


def on_mesh(fine):
    dp, tensor = ("y", "z"), ("x", "c")
    in_specs = (
        P(dp, tensor),
        P(dp, tensor),
        P(tensor, None),
        P(None, tensor),
        P(tensor, dp),
        P(tensor, dp),
        P(tensor, None),
        P(tensor, None),
    )
    out_specs = (P(None, tensor, dp), P(None, dp, tensor, None))
    return jax.shard_map(
        functools.partial(body, dp), mesh=fine, in_specs=in_specs, out_specs=out_specs, check_vma=False
    )
```

time: 152 us -> 97.5 us (0.64)
  waiting for transfers between devices: 83 us -> 18.3 us
  blocking collectives: 20.6 us -> 53.9 us
  between operations: 14.2 us -> 0.74 us
  starting transfers between devices: 22.6 us -> 16.3 us
  local copies, waits for them, and re-layouts: 2.21 us -> 0.03 us
  Pallas kernels: 9.45 us -> 7.85 us
    all_gather x1 -> x0, waiting for transfers between devices: 62.9 us -> none  [gather_moments(): return lax.all_gather(packed, dp, axis=0, tiled=True)]
    all_to_all x0 -> x2, blocking collectives: none -> 33.4 us  [the longest x1 19 us: body(): moments = lax.all_to_all(row_copies, dp[0], 0, 0)]
    all_to_all x1 -> x0, starting transfers between devices: 6.12 us -> none  [body(): grads = lax.all_to_all(send, dp, 0, 0)]
    unnamed x20 -> x12, local copies, waits for them, and re-layouts: 2.21 us -> 0.03 us
    all_to_all x1, waiting for transfers between devices: 18.6 us -> 17 us  [body(): mine = lax.all_to_all(chunks, dp, 0, 0)]
  transfers between devices with their start and end apart: 4 -> 2, of which waited for: 3 -> 2; matrix products, arithmetic and copies ran while one was open for 0% -> 0% of each run, Pallas kernels for 3% -> 2%
where the time goes in v2:
time: 97.5 us; the launch traced here: 97.1 us
  blocking collectives  53.9 us (55%)
  waiting for transfers between devices  18.3 us (19%)
  starting transfers between devices  16.3 us (17%)
  Pallas kernels  7.85 us (8%)
    all_to_all x1, blocking collectives, body(): parts = lax.all_to_all(copies, 'x', 0, 0)  20.6 us
    all_to_all x1, blocking collectives, body(): moments = lax.all_to_all(row_copies, dp[0], 0, 0)  19 us
    all_to_all x1, waiting for transfers between devices, body(): mine = lax.all_to_all(chunks, dp, 0, 0)  17 us
    all_to_all x1, blocking collectives, body(): row = lax.all_to_all(send, dp[1], 0, 0)  14.4 us
    all_to_all x1, starting transfers between devices, body(): mine = lax.all_to_all(chunks, dp, 0, 0)  14.4 us
    pallas_call x1, Pallas kernels, body(): pl.pallas_call(low_rank_kernel, out_shape=(jax.ShapeDtypeStruct((tokens,...  2.44 us
  transfers between devices with their start and end apart: 2, of which 2 were waited for; matrix products, arithmetic and copies ran while one was open for 0% of the time, Pallas kernels for 2%

profile of v2, /device:TPU:2, one launch (start us, length us, event | category | flops | bytes accessed | tf_op | source)
XLA Modules:
  0.0 97.1 jit_solution(6763869873451816218)
XLA Ops:
  0.6 2.4 %low_rank.1 = (bf16[512,128]{1,0:T(8,128)(2,1)S(1)}, bf16[512,1024]{1,0:T(8,128)(2,1)S(1)}, bf16[512,1024]{1,0:T(8,128)(2,1)S(1)}) custom-call(bf16[512,1024]{1,0:T(8,128)(2,1)} %act.1, bf16[512,1024]{1,0:T(8,128)(2,1)} %cot.1, f32[64,1024]{1,0:T(8,128)} %bitcast.6, f32[64,1024]{1,0:T(8,128)} %up.3), custom_call_target="tpu_custom_call" | custom-call | tf_op jit(solution)/shard_map/low_rank/pallas_call | solution.py:184
  3.1 1.9 %collective-permute-start = (bf16[512,128]{1,0:T(8,128)(2,1)S(1)}, bf16[512,128]{1,0:T(8,128)(2,1)S(1)}, u32[]{:S(2)}, u32[]{:S(2)}) collective-permute-start(bf16[512,128]{1,0:T(8,128)(2,1)S(1)} %get-tuple-element.9.mine), channel_id=1, source_target_pairs={{0,1},{1,0},{2,3},{3,2},{4,5},{5,4},{6,7},{7,6},{8,9},{9,8},{10,11... | collective-permute-start | bytes 393224 | tf_op jit(solution)/shard_map/ppermute | solution.py:201
  5.0 1.3 %collective-permute-done.other = bf16[512,128]{1,0:T(8,128)(2,1)S(1)} collective-permute-done((bf16[512,128]{1,0:T(8,128)(2,1)S(1)}, bf16[512,128]{1,0:T(8,128)(2,1)S(1)}, u32[]{:S(2)}, u32[]{:S(2)}) %collective-permute-start) | collective-permute-done | bytes 131104 | tf_op jit(solution)/shard_map/ppermute | solution.py:201
  6.4 20.6 %all_to_all.20.parts = bf16[4,512,128]{2,1,0:T(8,128)(2,1)S(1)} all-to-all(bf16[4,512,128]{2,1,0:T(8,128)(2,1)S(1)} %add_cores.1), channel_id=1, replica_groups=mesh['y'=8,'z'=12,'x'=4,'c'=2] {'x'}, dimensions={0} | all-to-all | bytes 1048576 | tf_op jit(solution)/shard_map/all_to_all | solution.py:222
  26.9 0.0 copy-start
  26.9 0.0 copy-start.1
  26.9 0.0 copy-start.4
  26.9 0.0 copy-start.5
  26.9 0.0 copy-start.2
  26.9 0.0 copy-start.3
  27.0 1.5 %grads.1 = bf16[96,4,384]{2,1,0:T(4,128)(2,1)} custom-call(bf16[4,512,128]{2,1,0:T(8,128)(2,1)S(1)} %all_to_all.20.parts, bf16[512,1024]{1,0:T(8,128)(2,1)S(1)} %get-tuple-element.10.act, bf16[512,1024]{1,0:T(8,128)(2,1)S(1)} %get-tuple-element.11.cot), custom_call_target="tpu_custom_call" | custom-call | tf_op jit(solution)/shard_map/grads/pallas_call | solution.py:223
  28.4 14.4 %all-to-all-start.1 = ((bf16[96,4,384]{2,1,0:T(4,128)(2,1)}), bf16[96,4,384]{2,1,0:T(4,128)(2,1)S(1)}, u32[]{:S(2)}, u32[]{:S(2)}) async-start(bf16[96,4,384]{2,1,0:T(4,128)(2,1)} %grads.1), calls=%async_computation.1 | async-start | bytes 589824 | tf_op jit(solution)/shard_map/all_to_all | solution.py:235
  42.8 0.0 copy-done
  42.8 0.0 copy-done.1
  42.9 0.0 copy-done.4
  42.9 0.0 copy-done.5
  42.9 1.7 %flat_param.1 = (f32[1064,128]{1,0:T(8,128)S(1)}, f32[1056,128]{1,0:T(8,128)S(1)}) custom-call(s32[1]{0:T(128)} %bitcast.me, s32[1,64]{1,0:T(1,128)S(1)} %copy-done.4, s32[1,64]{1,0:T(1,128)S(1)} %copy-done.5, f32[64,1024]{1,0:T(8,128)S(1)} %bitcast.7, f32[64,1024]{1,0:T(8,128)S(1)} %copy-done.1), custom_call_target="tpu_custom_call" | custom-call | tf_op jit(solution)/shard_map/flat_param/pallas_call | solution.py:202
  44.6 17.0 %all-to-all-done.1.parts = bf16[96,4,384]{2,1,0:T(4,128)(2,1)S(1)} async-done(((bf16[96,4,384]{2,1,0:T(4,128)(2,1)}), bf16[96,4,384]{2,1,0:T(4,128)(2,1)S(1)}, u32[]{:S(2)}, u32[]{:S(2)}) %all-to-all-start.1) | async-done | bytes 294944 | tf_op jit(solution)/shard_map/all_to_all | solution.py:235
  61.6 0.0 copy-done.2
  61.6 0.0 copy-done.3
  61.6 0.8 partition.1
  62.4 14.4 %all_to_all.21 = bf16[12,24,128]{2,1,0:T(8,128)(2,1)S(1)} all-to-all(bf16[12,24,128]{2,1,0:T(8,128)(2,1)S(1)} %get-tuple-element.14), channel_id=1, replica_groups=mesh['y'=8,'z'=12,'x'=4,'c'=2] {'z'}, dimensions={0} | all-to-all | bytes 147456 | tf_op jit(solution)/shard_map/all_to_all | solution.py:250
  76.8 0.1 row_copies.1
  76.9 19.0 %all_to_all.22 = bf16[8,288,128]{2,1,0:T(8,128)(2,1)S(1)} all-to-all(bf16[8,288,128]{2,1,0:T(8,128)(2,1)S(1)} %row_copies.1), channel_id=1, replica_groups=mesh['y'=8,'z'=12,'x'=4,'c'=2] {'y'}, dimensions={0} | all-to-all | bytes 1179648 | tf_op jit(solution)/shard_map/all_to_all | solution.py:259
  95.8 1.3 %written.1 = f32[3,1056,128]{2,1,0:T(8,128)} custom-call(bf16[96,24,128]{2,1,0:T(8,128)(2,1)S(1)} %bitcast.5, f32[1064,128]{1,0:T(8,128)S(1)} %get-tuple-element.12.flat, f32[1056,128]{1,0:T(8,128)S(1)} %get-tuple-element.15.mask), custom_call_target="tpu_custom_call" | custom-call | tf_op jit(solution)/shard_map/written/pallas_call | solution.py:260
  (1 shorter events, 0.0 us)
Async XLA Ops:
  3.1 3.2 %collective-permute-start = (bf16[512,128]{1,0:T(8,128)(2,1)S(1)}, bf16[512,128]{1,0:T(8,128)(2,1)S(1)}, u32[]{:S(2)}, u32[]{:S(2)}) collective-permute-start(bf16[512,128]{1,0:T(8,128)(2,1)S(1)} %get-tuple-element.9.mine), channel_id=1, source_target_pairs={{0,1},{1,0},{2,3},{3,2},{4,5},{5,4},{6,7},{7,6},{8,9},{9,8},{10,11... | collective-permute-start | bytes 393224 | tf_op jit(solution)/shard_map/ppermute | solution.py:201
  26.9 15.9 %copy-start = (f32[1024,64]{0,1:T(8,128)S(1)}, f32[1024,64]{0,1:T(8,128)}, u32[]{:S(2)}) copy-start(f32[1024,64]{0,1:T(8,128)} %param.10) | copy-start | bytes 786436
  26.9 15.9 %copy-start.1 = (f32[64,1024]{1,0:T(8,128)S(1)}, f32[64,1024]{1,0:T(8,128)}, u32[]{:S(2)}) copy-start(f32[64,1024]{1,0:T(8,128)} %up.3) | copy-start | bytes 786436
  26.9 15.9 %copy-start.4 = (s32[1,64]{1,0:T(1,128)S(1)}, s32[1,64]{1,0:T(1,128)}, u32[]{:S(2)}) copy-start(s32[1,64]{1,0:T(1,128)} %lengths.1) | copy-start | bytes 772
  26.9 15.9 %copy-start.5 = (s32[1,64]{1,0:T(1,128)S(1)}, s32[1,64]{1,0:T(1,128)}, u32[]{:S(2)}) copy-start(s32[1,64]{1,0:T(1,128)} %writers.1) | copy-start | bytes 772
  26.9 34.7 %copy-start.2 = (f32[1,1408]{1,0:T(1,128)S(1)}, f32[1,1408]{1,0:T(1,128)}, u32[]{:S(2)}) copy-start(f32[1,1408]{1,0:T(1,128)} %first.1) | copy-start | bytes 16900
  26.9 34.7 %copy-start.3 = (f32[1,1408]{1,0:T(1,128)S(1)}, f32[1,1408]{1,0:T(1,128)}, u32[]{:S(2)}) copy-start(f32[1,1408]{1,0:T(1,128)} %second.1) | copy-start | bytes 16900
  28.4 33.2 %all-to-all-start.1 = ((bf16[96,4,384]{2,1,0:T(4,128)(2,1)}), bf16[96,4,384]{2,1,0:T(4,128)(2,1)S(1)}, u32[]{:S(2)}, u32[]{:S(2)}) async-start(bf16[96,4,384]{2,1,0:T(4,128)(2,1)} %grads.1), calls=%async_computation.1 | async-start | bytes 589824 | tf_op jit(solution)/shard_map/all_to_all | solution.py:235

commit v3 on v2

--- a/solution.py
+++ b/solution.py
@@ -115,7 +115,7 @@
     return param - 0.01 * (fresh_one / fixed_one) / (jnp.sqrt(fresh_two / fixed_two) + 1e-08)
 
 
-def partition_kernel(rows, me, parts, flat, first, second, out, send, grad, one, two):
+def partition_kernel(rows, me, parts, flat, first, second, out, send, grad, one, two, both):
     total = jnp.sum(parts[...].astype(F32), axis=0)
     part = total.shape[0]
     half = grad.shape[0]
@@ -128,32 +128,42 @@
     one[rows:, :] = blank
     two[rows:, :] = blank
     fresh = adam_moments(grad[...], one[...], two[...])
-    both = jnp.concatenate(fresh, axis=0).astype(BF16)
+    for i in range(2):
+        for r in range(rows):
+            both[i : i + 1, r * LANES : (r + 1) * LANES] = fresh[i][r : r + 1, :]
+    packed = both[...].astype(BF16)
     for j in range(send.shape[0]):
-        send[j] = both
+        send[j] = packed
     updated = adam_param(flat[pl.ds(me[0] * rows, half), :], *fresh)
     for i, values in enumerate((updated,) + fresh):
         for r in range(rows):
             out[i, :, r * LANES : (r + 1) * LANES] = values[r : r + 1, :]
 
 
-def copies_kernel(source, out):
-    values = source[...]
-    for i in range(out.shape[0]):
-        out[i] = values
+def row_kernel(source, out, wide):
+    count = source.shape[0]
+    for z in range(count):
+        pair = source[z].astype(F32)
+        for i in range(2):
+            wide[i * count + z : i * count + z + 1, :] = pair[i : i + 1]
+    values = wide[...].astype(BF16)
+    for y in range(out.shape[0]):
+        out[y] = values
 
 
 def written_kernel(rows, moments, flat, mask, out, one, two, fresh, sems):
-    half = moments.shape[1] // 2
+    count = moments.shape[1] // 2
     steps = sems.shape[0]
     per_step = moments.shape[0] // steps
-    tall = per_step * rows
+    tall = per_step * count * rows
     copies = []
     for s in range(steps):
-        for j in range(s * per_step, (s + 1) * per_step):
-            values = moments[j].astype(F32)
-            one[rows * j : rows * j + half, :] = values[:half]
-            two[rows * j : rows * j + half, :] = values[half:]
+        for y in range(s * per_step, (s + 1) * per_step):
+            for r in range(rows):
+                values = moments[y, :, r * LANES : (r + 1) * LANES].astype(F32)
+                at = pl.ds(y * count * rows + r, count, stride=rows)
+                one[at, :] = values[:count]
+                two[at, :] = values[count:]
         for r in range(s * tall, (s + 1) * tall, 24):
             at = slice(r, r + 24)
             keep = mask[at, :] > 0.0
@@ -239,23 +249,24 @@
         functools.partial(partition_kernel, rows),
         out_shape=(
             jax.ShapeDtypeStruct((3, 1, part_len), F32),
-            jax.ShapeDtypeStruct((z_count, 2 * half, LANES), BF16),
+            jax.ShapeDtypeStruct((z_count, 2, part_len), BF16),
         ),
         in_specs=[SMEM] + [VMEM] * 4,
         out_specs=(VMEM, VMEM),
-        scratch_shapes=[pltpu.VMEM((half, LANES), F32)] * 3,
+        scratch_shapes=[pltpu.VMEM((half, LANES), F32)] * 3 + [pltpu.VMEM((2, part_len), F32)],
         compiler_params=PARAMS,
         name="partition",
     )(me, mine, flat_param, first_moment, second_moment)
     row = lax.all_to_all(send, dp[1], 0, 0)
     row_copies = pl.pallas_call(
-        copies_kernel,
-        out_shape=jax.ShapeDtypeStruct((lax.axis_size(dp[0]), z_count * 2 * half, LANES), BF16),
+        row_kernel,
+        out_shape=jax.ShapeDtypeStruct((lax.axis_size(dp[0]), 2 * z_count, part_len), BF16),
         in_specs=[VMEM],
         out_specs=VMEM,
+        scratch_shapes=[pltpu.VMEM((2 * z_count, part_len), F32)],
         compiler_params=PARAMS,
         name="row_copies",
-    )(row.reshape(z_count * 2 * half, LANES))
+    )(row)
     moments = lax.all_to_all(row_copies, dp[0], 0, 0)
     written = pl.pallas_call(
         functools.partial(written_kernel, rows),
@@ -263,14 +274,14 @@
         in_specs=[VMEM] * 3,
         out_specs=HBM,
         scratch_shapes=[
-            pltpu.VMEM((all_rows + 8, LANES), F32),
-            pltpu.VMEM((all_rows + 8, LANES), F32),
+            pltpu.VMEM((all_rows, LANES), F32),
+            pltpu.VMEM((all_rows, LANES), F32),
             pltpu.VMEM((3, all_rows, LANES), F32),
             pltpu.SemaphoreType.DMA((4,)),
         ],
         compiler_params=PARAMS,
         name="written",
-    )(moments.reshape(dp_count, 2 * half, LANES), flat_param, mask)
+    )(moments, flat_param, mask)
     return (partition, written.reshape(3, 1, 1, all_rows * LANES))
 
 

time: 97.5 us -> 96.4 us (0.989)
  blocking collectives: 53.9 us -> 52.8 us
    all_to_all x1, blocking collectives: 19 us -> 17.5 us  [body(): moments = lax.all_to_all(row_copies, dp[0], 0, 0)]
where the time goes in v3:
time: 96.4 us; the launch traced here: 96 us
  blocking collectives  52.8 us (55%)
  waiting for transfers between devices  18.3 us (19%)
  starting transfers between devices  16.3 us (17%)
  Pallas kernels  7.84 us (8%)
    all_to_all x1, blocking collectives, body(): parts = lax.all_to_all(copies, 'x', 0, 0)  20.6 us
    all_to_all x1, blocking collectives, body(): moments = lax.all_to_all(row_copies, dp[0], 0, 0)  17.5 us
    all_to_all x1, waiting for transfers between devices, body(): mine = lax.all_to_all(chunks, dp, 0, 0)  17 us
    all_to_all x1, blocking collectives, body(): row = lax.all_to_all(send, dp[1], 0, 0)  14.7 us
    all_to_all x1, starting transfers between devices, body(): mine = lax.all_to_all(chunks, dp, 0, 0)  14.4 us
    pallas_call x1, Pallas kernels, body(): pl.pallas_call(low_rank_kernel, out_shape=(jax.ShapeDtypeStruct((tokens,...  2.44 us
  transfers between devices with their start and end apart: 2, of which 2 were waited for; matrix products, arithmetic and copies ran while one was open for 0% of the time, Pallas kernels for 2%

profile of v3, /device:TPU:2, one launch (start us, length us, event | category | flops | bytes accessed | tf_op | source)
XLA Modules:
  0.0 96.0 jit_solution(11326524683669907904)
XLA Ops:
  0.6 2.4 %low_rank.1 = (bf16[512,128]{1,0:T(8,128)(2,1)S(1)}, bf16[512,1024]{1,0:T(8,128)(2,1)S(1)}, bf16[512,1024]{1,0:T(8,128)(2,1)S(1)}) custom-call(bf16[512,1024]{1,0:T(8,128)(2,1)} %act.1, bf16[512,1024]{1,0:T(8,128)(2,1)} %cot.1, f32[64,1024]{1,0:T(8,128)} %bitcast.3, f32[64,1024]{1,0:T(8,128)} %up.3), custom_call_target="tpu_custom_call" | custom-call | tf_op jit(solution)/shard_map/low_rank/pallas_call | solution.py:194
  3.1 1.9 %collective-permute-start = (bf16[512,128]{1,0:T(8,128)(2,1)S(1)}, bf16[512,128]{1,0:T(8,128)(2,1)S(1)}, u32[]{:S(2)}, u32[]{:S(2)}) collective-permute-start(bf16[512,128]{1,0:T(8,128)(2,1)S(1)} %get-tuple-element.9.mine), channel_id=1, source_target_pairs={{0,1},{1,0},{2,3},{3,2},{4,5},{5,4},{6,7},{7,6},{8,9},{9,8},{10,11... | collective-permute-start | bytes 393224 | tf_op jit(solution)/shard_map/ppermute | solution.py:211
  5.0 1.3 %collective-permute-done.other = bf16[512,128]{1,0:T(8,128)(2,1)S(1)} collective-permute-done((bf16[512,128]{1,0:T(8,128)(2,1)S(1)}, bf16[512,128]{1,0:T(8,128)(2,1)S(1)}, u32[]{:S(2)}, u32[]{:S(2)}) %collective-permute-start) | collective-permute-done | bytes 131104 | tf_op jit(solution)/shard_map/ppermute | solution.py:211
  6.4 20.6 %all_to_all.20.parts = bf16[4,512,128]{2,1,0:T(8,128)(2,1)S(1)} all-to-all(bf16[4,512,128]{2,1,0:T(8,128)(2,1)S(1)} %add_cores.1), channel_id=1, replica_groups=mesh['y'=8,'z'=12,'x'=4,'c'=2] {'x'}, dimensions={0} | all-to-all | bytes 1048576 | tf_op jit(solution)/shard_map/all_to_all | solution.py:232
  26.9 0.0 copy-start
  26.9 0.0 copy-start.1
  26.9 0.0 copy-start.4
  26.9 0.0 copy-start.5
  26.9 0.0 copy-start.2
  26.9 0.0 copy-start.3
  27.0 1.5 %grads.1 = bf16[96,4,384]{2,1,0:T(4,128)(2,1)} custom-call(bf16[4,512,128]{2,1,0:T(8,128)(2,1)S(1)} %all_to_all.20.parts, bf16[512,1024]{1,0:T(8,128)(2,1)S(1)} %get-tuple-element.10.act, bf16[512,1024]{1,0:T(8,128)(2,1)S(1)} %get-tuple-element.11.cot), custom_call_target="tpu_custom_call" | custom-call | tf_op jit(solution)/shard_map/grads/pallas_call | solution.py:233
  28.4 14.4 %all-to-all-start.1 = ((bf16[96,4,384]{2,1,0:T(4,128)(2,1)}), bf16[96,4,384]{2,1,0:T(4,128)(2,1)S(1)}, u32[]{:S(2)}, u32[]{:S(2)}) async-start(bf16[96,4,384]{2,1,0:T(4,128)(2,1)} %grads.1), calls=%async_computation.1 | async-start | bytes 589824 | tf_op jit(solution)/shard_map/all_to_all | solution.py:245
  42.8 0.0 copy-done
  42.8 0.0 copy-done.1
  42.9 0.0 copy-done.4
  42.9 0.0 copy-done.5
  42.9 1.7 %flat_param.1 = (f32[1064,128]{1,0:T(8,128)S(1)}, f32[1056,128]{1,0:T(8,128)S(1)}) custom-call(s32[1]{0:T(128)} %bitcast.me, s32[1,64]{1,0:T(1,128)S(1)} %copy-done.4, s32[1,64]{1,0:T(1,128)S(1)} %copy-done.5, f32[64,1024]{1,0:T(8,128)S(1)} %bitcast.4, f32[64,1024]{1,0:T(8,128)S(1)} %copy-done.1), custom_call_target="tpu_custom_call" | custom-call | tf_op jit(solution)/shard_map/flat_param/pallas_call | solution.py:212
  44.6 17.0 %all-to-all-done.1.parts = bf16[96,4,384]{2,1,0:T(4,128)(2,1)S(1)} async-done(((bf16[96,4,384]{2,1,0:T(4,128)(2,1)}), bf16[96,4,384]{2,1,0:T(4,128)(2,1)S(1)}, u32[]{:S(2)}, u32[]{:S(2)}) %all-to-all-start.1) | async-done | bytes 294944 | tf_op jit(solution)/shard_map/all_to_all | solution.py:245
  61.6 0.0 copy-done.2
  61.6 0.0 copy-done.3
  61.6 0.8 partition.1
  62.4 14.7 %all_to_all.21.source = bf16[12,2,1408]{2,1,0:T(2,128)(2,1)S(1)} all-to-all(bf16[12,2,1408]{2,1,0:T(2,128)(2,1)S(1)} %get-tuple-element.14), channel_id=1, replica_groups=mesh['y'=8,'z'=12,'x'=4,'c'=2] {'z'}, dimensions={0} | all-to-all | bytes 135168 | tf_op jit(solution)/shard_map/all_to_all | solution.py:260
  77.1 0.1 row_copies.1
  77.2 17.5 %all_to_all.22.moments = bf16[8,24,1408]{2,1,0:T(8,128)(2,1)S(1)} all-to-all(bf16[8,24,1408]{2,1,0:T(8,128)(2,1)S(1)} %row_copies.1), channel_id=1, replica_groups=mesh['y'=8,'z'=12,'x'=4,'c'=2] {'y'}, dimensions={0} | all-to-all | bytes 1081344 | tf_op jit(solution)/shard_map/all_to_all | solution.py:270
  94.7 1.3 %written.1 = f32[3,1056,128]{2,1,0:T(8,128)} custom-call(bf16[8,24,1408]{2,1,0:T(8,128)(2,1)S(1)} %all_to_all.22.moments, f32[1064,128]{1,0:T(8,128)S(1)} %get-tuple-element.12.flat, f32[1056,128]{1,0:T(8,128)S(1)} %get-tuple-element.15.mask), custom_call_target="tpu_custom_call" | custom-call | tf_op jit(solution)/shard_map/written/pallas_call | solution.py:271
  (1 shorter events, 0.0 us)
Async XLA Ops:
  3.1 3.2 %collective-permute-start = (bf16[512,128]{1,0:T(8,128)(2,1)S(1)}, bf16[512,128]{1,0:T(8,128)(2,1)S(1)}, u32[]{:S(2)}, u32[]{:S(2)}) collective-permute-start(bf16[512,128]{1,0:T(8,128)(2,1)S(1)} %get-tuple-element.9.mine), channel_id=1, source_target_pairs={{0,1},{1,0},{2,3},{3,2},{4,5},{5,4},{6,7},{7,6},{8,9},{9,8},{10,11... | collective-permute-start | bytes 393224 | tf_op jit(solution)/shard_map/ppermute | solution.py:211
  26.9 15.9 %copy-start = (f32[1024,64]{0,1:T(8,128)S(1)}, f32[1024,64]{0,1:T(8,128)}, u32[]{:S(2)}) copy-start(f32[1024,64]{0,1:T(8,128)} %param.10) | copy-start | bytes 786436
  26.9 15.9 %copy-start.1 = (f32[64,1024]{1,0:T(8,128)S(1)}, f32[64,1024]{1,0:T(8,128)}, u32[]{:S(2)}) copy-start(f32[64,1024]{1,0:T(8,128)} %up.3) | copy-start | bytes 786436
  26.9 15.9 %copy-start.4 = (s32[1,64]{1,0:T(1,128)S(1)}, s32[1,64]{1,0:T(1,128)}, u32[]{:S(2)}) copy-start(s32[1,64]{1,0:T(1,128)} %lengths.1) | copy-start | bytes 772
  26.9 15.9 %copy-start.5 = (s32[1,64]{1,0:T(1,128)S(1)}, s32[1,64]{1,0:T(1,128)}, u32[]{:S(2)}) copy-start(s32[1,64]{1,0:T(1,128)} %writers.1) | copy-start | bytes 772
  26.9 34.7 %copy-start.2 = (f32[1,1408]{1,0:T(1,128)S(1)}, f32[1,1408]{1,0:T(1,128)}, u32[]{:S(2)}) copy-start(f32[1,1408]{1,0:T(1,128)} %first.1) | copy-start | bytes 16900
  26.9 34.7 %copy-start.3 = (f32[1,1408]{1,0:T(1,128)S(1)}, f32[1,1408]{1,0:T(1,128)}, u32[]{:S(2)}) copy-start(f32[1,1408]{1,0:T(1,128)} %second.1) | copy-start | bytes 16900
  28.4 33.2 %all-to-all-start.1 = ((bf16[96,4,384]{2,1,0:T(4,128)(2,1)}), bf16[96,4,384]{2,1,0:T(4,128)(2,1)S(1)}, u32[]{:S(2)}, u32[]{:S(2)}) async-start(bf16[96,4,384]{2,1,0:T(4,128)(2,1)} %grads.1), calls=%async_computation.1 | async-start | bytes 589824 | tf_op jit(solution)/shard_map/all_to_all | solution.py:245

commit v4 on v3

--- a/solution.py
+++ b/solution.py
@@ -37,7 +37,7 @@
     out[...] = both.astype(BF16)
 
 
-def add_copies_kernel(mine, other, out):
+def add_copies_kernel(mine, other, after, out):
     total = (mine[...].astype(F32) + other[...].astype(F32)).astype(BF16)
     for i in range(out.shape[0]):
         out[i] = total
@@ -84,7 +84,7 @@
 
         return end
 
-    lax.fori_loop(0, lengths.shape[1], piece, 0)
+    lax.fori_loop(0, lengths.shape[1], piece, 0, unroll=8)
 
 
 def grad_kernel(rows, parts, act, cot, out, flat, wide):
@@ -115,29 +115,29 @@
     return param - 0.01 * (fresh_one / fixed_one) / (jnp.sqrt(fresh_two / fixed_two) + 1e-08)
 
 
-def partition_kernel(rows, me, parts, flat, first, second, out, send, grad, one, two, both):
-    total = jnp.sum(parts[...].astype(F32), axis=0)
-    part = total.shape[0]
-    half = grad.shape[0]
-    for i in range(total.shape[1] // LANES):
-        grad[part * i : part * (i + 1), :] = total[:, i * LANES : (i + 1) * LANES]
+def own_moments(rows, first, second, one, two):
     for r in range(rows):
         one[r : r + 1, :] = first[:, r * LANES : (r + 1) * LANES]
         two[r : r + 1, :] = second[:, r * LANES : (r + 1) * LANES]
-    blank = jnp.zeros((half - rows, LANES), F32)
+    blank = jnp.zeros((one.shape[0] - rows, LANES), F32)
     one[rows:, :] = blank
     two[rows:, :] = blank
+
+
+def owner_kernel(rows, parts, first, second, fresh_one, fresh_two, send, grad, one, two, both):
+    total = jnp.sum(parts[...].astype(F32), axis=0)
+    part = total.shape[0]
+    for i in range(total.shape[1] // LANES):
+        grad[part * i : part * (i + 1), :] = total[:, i * LANES : (i + 1) * LANES]
+    own_moments(rows, first, second, one, two)
     fresh = adam_moments(grad[...], one[...], two[...])
+    fresh_one[...], fresh_two[...] = fresh
     for i in range(2):
         for r in range(rows):
             both[i : i + 1, r * LANES : (r + 1) * LANES] = fresh[i][r : r + 1, :]
     packed = both[...].astype(BF16)
     for j in range(send.shape[0]):
         send[j] = packed
-    updated = adam_param(flat[pl.ds(me[0] * rows, half), :], *fresh)
-    for i, values in enumerate((updated,) + fresh):
-        for r in range(rows):
-            out[i, :, r * LANES : (r + 1) * LANES] = values[r : r + 1, :]
 
 
 def row_kernel(source, out, wide):
@@ -151,12 +151,18 @@
         out[y] = values
 
 
-def written_kernel(rows, moments, flat, mask, out, one, two, fresh, sems):
+def written_kernel(rows, me, own_one, own_two, moments, flat, mask, own, out, one, two, fresh, mine, sems):
     count = moments.shape[1] // 2
-    steps = sems.shape[0]
+    steps = sems.shape[0] - 1
     per_step = moments.shape[0] // steps
     tall = per_step * count * rows
-    copies = []
+    values = own_one[...], own_two[...]
+    values = (adam_param(flat[pl.ds(me[0] * rows, own_one.shape[0]), :], *values),) + values
+    for i in range(3):
+        for r in range(rows):
+            mine[i, :, r * LANES : (r + 1) * LANES] = values[i][r : r + 1, :]
+    copies = [pltpu.make_async_copy(mine, own, sems.at[steps])]
+    copies[0].start()
     for s in range(steps):
         for y in range(s * per_step, (s + 1) * per_step):
             for r in range(rows):
@@ -224,11 +230,11 @@
     copies = pl.pallas_call(
         add_copies_kernel,
         out_shape=jax.ShapeDtypeStruct((x_count, tokens, 2 * rank), BF16),
-        in_specs=[VMEM] * 2,
+        in_specs=[VMEM, VMEM, pl.BlockSpec(memory_space=pl.ANY)],
         out_specs=VMEM,
         compiler_params=PARAMS,
         name="add_cores",
-    )(partial, other)
+    )(partial, other, mask)
     parts = lax.all_to_all(copies, "x", 0, 0)
     chunks = pl.pallas_call(
         functools.partial(grad_kernel, rows),
@@ -245,18 +251,19 @@
     mine = lax.all_to_all(chunks, dp, 0, 0)
     half = lanes * part // LANES
     z_count = lax.axis_size(dp[1])
-    partition, send = pl.pallas_call(
-        functools.partial(partition_kernel, rows),
+    own_one, own_two, send = pl.pallas_call(
+        functools.partial(owner_kernel, rows),
         out_shape=(
-            jax.ShapeDtypeStruct((3, 1, part_len), F32),
+            jax.ShapeDtypeStruct((half, LANES), F32),
+            jax.ShapeDtypeStruct((half, LANES), F32),
             jax.ShapeDtypeStruct((z_count, 2, part_len), BF16),
         ),
-        in_specs=[SMEM] + [VMEM] * 4,
-        out_specs=(VMEM, VMEM),
+        in_specs=[VMEM] * 3,
+        out_specs=(VMEM, VMEM, VMEM),
         scratch_shapes=[pltpu.VMEM((half, LANES), F32)] * 3 + [pltpu.VMEM((2, part_len), F32)],
         compiler_params=PARAMS,
-        name="partition",
-    )(me, mine, flat_param, first_moment, second_moment)
+        name="owner",
+    )(mine, first_moment, second_moment)
     row = lax.all_to_all(send, dp[1], 0, 0)
     row_copies = pl.pallas_call(
         row_kernel,
@@ -268,20 +275,24 @@
         name="row_copies",
     )(row)
     moments = lax.all_to_all(row_copies, dp[0], 0, 0)
-    written = pl.pallas_call(
+    partition, written = pl.pallas_call(
         functools.partial(written_kernel, rows),
-        out_shape=jax.ShapeDtypeStruct((3, all_rows, LANES), F32),
-        in_specs=[VMEM] * 3,
-        out_specs=HBM,
+        out_shape=(
+            jax.ShapeDtypeStruct((3, 1, part_len), F32),
+            jax.ShapeDtypeStruct((3, all_rows, LANES), F32),
+        ),
+        in_specs=[SMEM] + [VMEM] * 5,
+        out_specs=(HBM, HBM),
         scratch_shapes=[
             pltpu.VMEM((all_rows, LANES), F32),
             pltpu.VMEM((all_rows, LANES), F32),
             pltpu.VMEM((3, all_rows, LANES), F32),
-            pltpu.SemaphoreType.DMA((4,)),
+            pltpu.VMEM((3, 1, part_len), F32),
+            pltpu.SemaphoreType.DMA((5,)),
         ],
         compiler_params=PARAMS,
         name="written",
-    )(moments, flat_param, mask)
+    )(me, own_one, own_two, moments, flat_param, mask)
     return (partition, written.reshape(3, 1, 1, all_rows * LANES))
 
 

time: 96.4 us -> 96.5 us (level)
  blocking collectives: 52.8 us -> 87.2 us
  waiting for transfers between devices: 18.3 us -> 0.01 us
  starting transfers between devices: 16.3 us -> 1.92 us
  Pallas kernels: 7.84 us -> 6.31 us
    all_to_all x0 -> x1, blocking collectives: none -> 33.6 us  [body(): mine = lax.all_to_all(chunks, dp, 0, 0)]
    all_to_all x1 -> x0, waiting for transfers between devices: 17 us -> none  [body(): mine = lax.all_to_all(chunks, dp, 0, 0)]
    all_to_all x1 -> x0, starting transfers between devices: 14.4 us -> none  [body(): mine = lax.all_to_all(chunks, dp, 0, 0)]
    ppermute x1, waiting for transfers between devices: 1.31 us -> 0.01 us  [body(): other = lax.ppermute(partial, 'c', [(0, 1), (1, 0)])]
  transfers between devices with their start and end apart: 2 -> 1, of which waited for: 2 -> 0; matrix products, arithmetic and copies ran while one was open for 0% -> 0% of each run, Pallas kernels for 2% -> 2%
where the time goes in v4:
time: 96.5 us; the launch traced here: 96.2 us
  blocking collectives  87.2 us (90%)
  Pallas kernels  6.31 us (7%)
  starting transfers between devices  1.92 us (2%)
    all_to_all x1, blocking collectives, body(): mine = lax.all_to_all(chunks, dp, 0, 0)  33.6 us
    all_to_all x1, blocking collectives, body(): parts = lax.all_to_all(copies, 'x', 0, 0)  20.9 us
    all_to_all x1, blocking collectives, body(): moments = lax.all_to_all(row_copies, dp[0], 0, 0)  17.9 us
    all_to_all x1, blocking collectives, body(): row = lax.all_to_all(send, dp[1], 0, 0)  14.9 us
    pallas_call x1, Pallas kernels, body(): pl.pallas_call(low_rank_kernel, out_shape=(jax.ShapeDtypeStruct((tokens,...  2.48 us
  transfers between devices with their start and end apart: 1, of which 0 were waited for; matrix products, arithmetic and copies ran while one was open for 0% of the time, Pallas kernels for 2%

profile of v4, /device:TPU:2, one launch (start us, length us, event | category | flops | bytes accessed | tf_op | source)
XLA Modules:
  0.0 96.2 jit_solution(2462532373614340153)
XLA Ops:
  0.6 0.0 copy-start.1
  0.6 0.0 copy-start
  0.7 0.0 copy-start.5
  0.7 0.0 copy-start.4
  0.7 2.5 %low_rank.1 = (bf16[512,128]{1,0:T(8,128)(2,1)S(1)}, bf16[512,1024]{1,0:T(8,128)(2,1)S(1)}, bf16[512,1024]{1,0:T(8,128)(2,1)S(1)}) custom-call(bf16[512,1024]{1,0:T(8,128)(2,1)} %act.1, bf16[512,1024]{1,0:T(8,128)(2,1)} %cot.1, f32[64,1024]{1,0:T(8,128)} %bitcast.3, f32[64,1024]{1,0:T(8,128)} %up.3), custom_call_target="tpu_custom_call" | custom-call | tf_op jit(solution)/shard_map/low_rank/pallas_call | solution.py:200
  3.2 1.9 %collective-permute-start = (bf16[512,128]{1,0:T(8,128)(2,1)S(1)}, bf16[512,128]{1,0:T(8,128)(2,1)S(1)}, u32[]{:S(2)}, u32[]{:S(2)}) collective-permute-start(bf16[512,128]{1,0:T(8,128)(2,1)S(1)} %get-tuple-element.12.mine), channel_id=1, source_target_pairs={{0,1},{1,0},{2,3},{3,2},{4,5},{5,4},{6,7},{7,6},{8,9},{9,8},{10,11... | collective-permute-start | bytes 393224 | tf_op jit(solution)/shard_map/ppermute | solution.py:217
  5.1 0.0 copy-done.1
  5.1 0.0 copy-done
  5.1 0.0 copy-done.5
  5.1 0.0 copy-done.4
  5.1 1.5 %flat_param.1 = (f32[1064,128]{1,0:T(8,128)S(1)}, f32[1056,128]{1,0:T(8,128)S(1)}) custom-call(s32[1]{0:T(128)} %bitcast.me, s32[1,64]{1,0:T(1,128)S(1)} %copy-done.4, s32[1,64]{1,0:T(1,128)S(1)} %copy-done.5, f32[64,1024]{1,0:T(8,128)S(1)} %bitcast.4, f32[64,1024]{1,0:T(8,128)S(1)} %copy-done.1), custom_call_target="tpu_custom_call" | custom-call | tf_op jit(solution)/shard_map/flat_param/pallas_call | solution.py:218
  6.6 0.0 collective-permute-done.other
  6.7 20.9 %all_to_all.20.parts = bf16[4,512,128]{2,1,0:T(8,128)(2,1)S(1)} all-to-all(bf16[4,512,128]{2,1,0:T(8,128)(2,1)S(1)} %add_cores.1), channel_id=1, replica_groups=mesh['y'=8,'z'=12,'x'=4,'c'=2] {'x'}, dimensions={0} | all-to-all | bytes 1048576 | tf_op jit(solution)/shard_map/all_to_all | solution.py:238
  27.6 0.0 copy-start.2
  27.6 0.0 copy-start.3
  27.6 0.7 grads.1
  28.3 33.6 %all_to_all.21.parts = bf16[96,4,384]{2,1,0:T(4,128)(2,1)S(1)} all-to-all(bf16[96,4,384]{2,1,0:T(4,128)(2,1)S(1)} %grads.1), channel_id=1, replica_groups=mesh['y'=8,'z'=12,'x'=4,'c'=2] {'y','z'}, dimensions={0} | all-to-all | bytes 589824 | tf_op jit(solution)/shard_map/all_to_all | solution.py:251
  61.9 0.0 copy-done.2
  61.9 0.0 copy-done.3
  61.9 0.2 owner.1
  62.0 14.9 %all_to_all.22.source = bf16[12,2,1408]{2,1,0:T(2,128)(2,1)S(1)} all-to-all(bf16[12,2,1408]{2,1,0:T(2,128)(2,1)S(1)} %get-tuple-element.18), channel_id=1, replica_groups=mesh['y'=8,'z'=12,'x'=4,'c'=2] {'z'}, dimensions={0} | all-to-all | bytes 135168 | tf_op jit(solution)/shard_map/all_to_all | solution.py:267
  76.9 0.1 row_copies.1
  77.0 17.9 %all_to_all.23.moments = bf16[8,24,1408]{2,1,0:T(8,128)(2,1)S(1)} all-to-all(bf16[8,24,1408]{2,1,0:T(8,128)(2,1)S(1)} %row_copies.1), channel_id=1, replica_groups=mesh['y'=8,'z'=12,'x'=4,'c'=2] {'y'}, dimensions={0} | all-to-all | bytes 1081344 | tf_op jit(solution)/shard_map/all_to_all | solution.py:277
  94.8 1.3 %written.1 = (f32[3,1,1408]{2,1,0:T(1,128)}, f32[3,1056,128]{2,1,0:T(8,128)}) custom-call(s32[1]{0:T(128)} %bitcast.me, f32[12,128]{1,0:T(8,128)S(1)} %get-tuple-element.16.own_one, f32[12,128]{1,0:T(8,128)S(1)} %get-tuple-element.17.own_two, bf16[8,24,1408]{2,1,0:T(8,128)(2,1)S(1)} %all_to_all.23.moments, f32[1064,128]{1,0:T(8,128)S(1)} %get-tuple-element.19.flat, ...), custom_call_target="tpu_custom_call" | custom-call | tf_op jit(solution)/shard_map/written/pallas_call | solution.py:278
  (1 shorter events, 0.0 us)
Async XLA Ops:
  0.6 4.5 %copy-start.1 = (f32[64,1024]{1,0:T(8,128)S(1)}, f32[64,1024]{1,0:T(8,128)}, u32[]{:S(2)}) copy-start(f32[64,1024]{1,0:T(8,128)} %up.3) | copy-start | bytes 786436
  0.6 4.5 %copy-start = (f32[1024,64]{0,1:T(8,128)S(1)}, f32[1024,64]{0,1:T(8,128)}, u32[]{:S(2)}) copy-start(f32[1024,64]{0,1:T(8,128)} %param.10) | copy-start | bytes 786436
  0.7 4.5 %copy-start.5 = (s32[1,64]{1,0:T(1,128)S(1)}, s32[1,64]{1,0:T(1,128)}, u32[]{:S(2)}) copy-start(s32[1,64]{1,0:T(1,128)} %writers.1) | copy-start | bytes 772
  0.7 4.5 %copy-start.4 = (s32[1,64]{1,0:T(1,128)S(1)}, s32[1,64]{1,0:T(1,128)}, u32[]{:S(2)}) copy-start(s32[1,64]{1,0:T(1,128)} %lengths.1) | copy-start | bytes 772
  3.2 3.5 %collective-permute-start = (bf16[512,128]{1,0:T(8,128)(2,1)S(1)}, bf16[512,128]{1,0:T(8,128)(2,1)S(1)}, u32[]{:S(2)}, u32[]{:S(2)}) collective-permute-start(bf16[512,128]{1,0:T(8,128)(2,1)S(1)} %get-tuple-element.12.mine), channel_id=1, source_target_pairs={{0,1},{1,0},{2,3},{3,2},{4,5},{5,4},{6,7},{7,6},{8,9},{9,8},{10,11... | collective-permute-start | bytes 393224 | tf_op jit(solution)/shard_map/ppermute | solution.py:217
  27.6 34.3 %copy-start.2 = (f32[1,1408]{1,0:T(1,128)S(1)}, f32[1,1408]{1,0:T(1,128)}, u32[]{:S(2)}) copy-start(f32[1,1408]{1,0:T(1,128)} %first.1) | copy-start | bytes 16900
  27.6 34.3 %copy-start.3 = (f32[1,1408]{1,0:T(1,128)S(1)}, f32[1,1408]{1,0:T(1,128)}, u32[]{:S(2)}) copy-start(f32[1,1408]{1,0:T(1,128)} %second.1) | copy-start | bytes 16900

commit v5 on v4

--- a/solution.py
+++ b/solution.py
@@ -12,35 +12,8 @@
 LANES = 128
 VMEM = pl.BlockSpec(memory_space=pltpu.VMEM)
 HBM = pl.BlockSpec(memory_space=pltpu.HBM)
-SMEM = pl.BlockSpec(memory_space=pltpu.SMEM)
 NT = (((1,), (1,)), ((), ()))
 PARAMS = pltpu.CompilerParams(vmem_limit_bytes=16 * 1024 * 1024)
-
-
-def low_rank_kernel(act, cot, down_t, up, out, a, c, d, u, sems):
-    copies = [
-        pltpu.make_async_copy(source, target, sems.at[i])
-        for i, (source, target) in enumerate(((down_t, d), (act, a), (up, u), (cot, c)))
-    ]
-    for copy in copies:
-        copy.start()
-    copies[0].wait()
-    down_b = d[...].astype(BF16)
-    blank = jnp.zeros_like(down_b)
-    left = jnp.concatenate([down_b, blank], axis=0)
-    copies[1].wait()
-    both = lax.dot_general(a[...], left, NT, preferred_element_type=F32)
-    copies[2].wait()
-    right = jnp.concatenate([blank, u[...].astype(BF16)], axis=0)
-    copies[3].wait()
-    both += lax.dot_general(c[...], right, NT, preferred_element_type=F32)
-    out[...] = both.astype(BF16)
-
-
-def add_copies_kernel(mine, other, after, out):
-    total = (mine[...].astype(F32) + other[...].astype(F32)).astype(BF16)
-    for i in range(out.shape[0]):
-        out[i] = total
 
 
 def store_flat(flat, wide, down_t2, up):
@@ -59,9 +32,8 @@
     flat[used:, :] = jnp.zeros((flat.shape[0] - used, LANES), F32)
 
 
-def param_kernel(me, lengths, writers, down_t, up, flat, mask, wide):
-    left = down_t[...]
-    store_flat(flat, wide, jnp.concatenate([left, left], axis=0), up[...])
+def mark_pieces(dp, lengths, writers, mask):
+    me = lax.axis_index(dp)
     mask[...] = jnp.zeros_like(mask)
     block = 8 * LANES
     spot = lax.broadcasted_iota(jnp.int32, (8, LANES), 0) * LANES + lax.broadcasted_iota(
@@ -71,7 +43,7 @@
     def piece(k, start):
         end = start + lengths[0, k]
 
-        @pl.when(writers[0, k] == me[0])
+        @pl.when(writers[0, k] == me)
         def _():
             def mark(b, carry):
                 here = spot + b * block
@@ -84,7 +56,49 @@
 
         return end
 
-    lax.fori_loop(0, lengths.shape[1], piece, 0, unroll=8)
+    group = 8
+    begin = jnp.int32(0)
+    for low in range(0, lengths.shape[1], group):
+        hit = writers[0, low] == me
+        total = lengths[0, low]
+        for k in range(low + 1, low + group):
+            hit = jnp.logical_or(hit, writers[0, k] == me)
+            total += lengths[0, k]
+
+        @pl.when(hit)
+        def _(low=low, begin=begin):
+            lax.fori_loop(low, low + group, piece, begin)
+
+        begin += total
+
+
+def low_rank_kernel(
+    dp, act, cot, down_t, up, lengths, writers, out, a, c, flat, mask, d, u, wide, long, who, sems
+):
+    pairs = ((down_t, d), (up, u), (act, a), (cot, c), (lengths, long), (writers, who))
+    copies = [pltpu.make_async_copy(source, target, sems.at[i]) for i, (source, target) in enumerate(pairs)]
+    for copy in copies:
+        copy.start()
+    copies[0].wait()
+    copies[1].wait()
+    left, right = d[...], u[...]
+    store_flat(flat, wide, jnp.concatenate([left, left], axis=0), right)
+    down_b, up_b = left.astype(BF16), right.astype(BF16)
+    blank = jnp.zeros_like(down_b)
+    copies[4].wait()
+    copies[5].wait()
+    mark_pieces(dp, long, who, mask)
+    copies[2].wait()
+    both = lax.dot_general(a[...], jnp.concatenate([down_b, blank], axis=0), NT, preferred_element_type=F32)
+    copies[3].wait()
+    both += lax.dot_general(c[...], jnp.concatenate([blank, up_b], axis=0), NT, preferred_element_type=F32)
+    out[...] = both.astype(BF16)
+
+
+def add_copies_kernel(mine, other, out):
+    total = (mine[...].astype(F32) + other[...].astype(F32)).astype(BF16)
+    for i in range(out.shape[0]):
+        out[i] = total
 
 
 def grad_kernel(rows, parts, act, cot, out, flat, wide):
@@ -151,13 +165,13 @@
         out[y] = values
 
 
-def written_kernel(rows, me, own_one, own_two, moments, flat, mask, own, out, one, two, fresh, mine, sems):
+def written_kernel(rows, dp, own_one, own_two, moments, flat, mask, own, out, one, two, fresh, mine, sems):
     count = moments.shape[1] // 2
     steps = sems.shape[0] - 1
     per_step = moments.shape[0] // steps
     tall = per_step * count * rows
     values = own_one[...], own_two[...]
-    values = (adam_param(flat[pl.ds(me[0] * rows, own_one.shape[0]), :], *values),) + values
+    values = (adam_param(flat[pl.ds(lax.axis_index(dp) * rows, own_one.shape[0]), :], *values),) + values
     for i in range(3):
         for r in range(rows):
             mine[i, :, r * LANES : (r + 1) * LANES] = values[i][r : r + 1, :]
@@ -193,48 +207,41 @@
     lanes = -(-rows // part) * LANES
     tokens, width = activations.shape
     rank = factor_up.shape[0]
-    me = lax.axis_index(dp).astype(jnp.int32).reshape(1)
     down_t = factor_down.T
     x_count = lax.axis_size("x")
 
-    partial, act_copy, cot_copy = pl.pallas_call(
-        low_rank_kernel,
+    first_in = (activations, cotangent, down_t, factor_up, piece_lengths, writers)
+    partial, act_copy, cot_copy, flat_param, mask = pl.pallas_call(
+        functools.partial(low_rank_kernel, dp),
         out_shape=(
             jax.ShapeDtypeStruct((tokens, 2 * rank), BF16),
             jax.ShapeDtypeStruct((tokens, width), BF16),
             jax.ShapeDtypeStruct((tokens, width), BF16),
+            jax.ShapeDtypeStruct((all_rows + 8, LANES), F32),
+            jax.ShapeDtypeStruct((all_rows, LANES), F32),
         ),
-        in_specs=[HBM] * 4,
-        out_specs=(VMEM, VMEM, VMEM),
+        in_specs=[HBM] * 6,
+        out_specs=[VMEM] * 5,
         scratch_shapes=[
             pltpu.VMEM((rank, width), F32),
             pltpu.VMEM((rank, width), F32),
-            pltpu.SemaphoreType.DMA((4,)),
+            pltpu.VMEM((width, LANES), F32),
+            pltpu.SMEM(piece_lengths.shape, jnp.int32),
+            pltpu.SMEM(writers.shape, jnp.int32),
+            pltpu.SemaphoreType.DMA((6,)),
         ],
         compiler_params=PARAMS,
         name="low_rank",
-    )(*[pltpu.with_memory_space_constraint(v, pltpu.HBM) for v in (activations, cotangent, down_t, factor_up)])
+    )(*[pltpu.with_memory_space_constraint(v, pltpu.HBM) for v in first_in])
     other = lax.ppermute(partial, "c", [(0, 1), (1, 0)])
-    flat_param, mask = pl.pallas_call(
-        param_kernel,
-        out_shape=(
-            jax.ShapeDtypeStruct((all_rows + 8, LANES), F32),
-            jax.ShapeDtypeStruct((all_rows, LANES), F32),
-        ),
-        in_specs=[SMEM] * 3 + [VMEM] * 2,
-        out_specs=(VMEM, VMEM),
-        scratch_shapes=[pltpu.VMEM((width, LANES), F32)],
-        compiler_params=PARAMS,
-        name="flat_param",
-    )(me, piece_lengths, writers, down_t, factor_up)
     copies = pl.pallas_call(
         add_copies_kernel,
         out_shape=jax.ShapeDtypeStruct((x_count, tokens, 2 * rank), BF16),
-        in_specs=[VMEM, VMEM, pl.BlockSpec(memory_space=pl.ANY)],
+        in_specs=[VMEM] * 2,
         out_specs=VMEM,
         compiler_params=PARAMS,
         name="add_cores",
-    )(partial, other, mask)
+    )(partial, other)
     parts = lax.all_to_all(copies, "x", 0, 0)
     chunks = pl.pallas_call(
         functools.partial(grad_kernel, rows),
@@ -276,12 +283,12 @@
     )(row)
     moments = lax.all_to_all(row_copies, dp[0], 0, 0)
     partition, written = pl.pallas_call(
-        functools.partial(written_kernel, rows),
+        functools.partial(written_kernel, rows, dp),
         out_shape=(
             jax.ShapeDtypeStruct((3, 1, part_len), F32),
             jax.ShapeDtypeStruct((3, all_rows, LANES), F32),
         ),
-        in_specs=[SMEM] + [VMEM] * 5,
+        in_specs=[VMEM] * 5,
         out_specs=(HBM, HBM),
         scratch_shapes=[
             pltpu.VMEM((all_rows, LANES), F32),
@@ -292,7 +299,7 @@
         ],
         compiler_params=PARAMS,
         name="written",
-    )(me, own_one, own_two, moments, flat_param, mask)
+    )(own_one, own_two, moments, flat_param, mask)
     return (partition, written.reshape(3, 1, 1, all_rows * LANES))
 
 

time: 96.5 us -> 94.8 us (0.982)
  Pallas kernels: 6.31 us -> 4.8 us
  blocking collectives: 87.2 us -> 85.8 us
  waiting for transfers between devices: 0.01 us -> 1.31 us
    pallas_call x3 -> x2, Pallas kernels: 5.29 us -> 3.79 us  [the longest x1 2.45 us: body(): pl.pallas_call(functools.partial(low_rank_kernel, dp), out_shape=(jax.Sha...]
    ppermute x1, waiting for transfers between devices: 0.01 us -> 1.31 us  [body(): other = lax.ppermute(partial, 'c', [(0, 1), (1, 0)])]
  transfers between devices with their start and end apart: 1 -> 1, of which waited for: 0 -> 1; matrix products, arithmetic and copies ran while one was open for 0% -> 0% of each run, Pallas kernels for 2% -> 0%
where the time goes in v5:
time: 94.8 us; the launch traced here: 94.5 us
  blocking collectives  85.8 us (91%)
  Pallas kernels  4.8 us (5%)
  starting transfers between devices  1.92 us (2%)
  waiting for transfers between devices  1.31 us (1%)
    all_to_all x1, blocking collectives, body(): mine = lax.all_to_all(chunks, dp, 0, 0)  33 us
    all_to_all x1, blocking collectives, body(): parts = lax.all_to_all(copies, 'x', 0, 0)  20.6 us
    all_to_all x1, blocking collectives, body(): moments = lax.all_to_all(row_copies, dp[0], 0, 0)  17.5 us
    all_to_all x1, blocking collectives, body(): row = lax.all_to_all(send, dp[1], 0, 0)  14.8 us
    pallas_call x1, Pallas kernels, body(): pl.pallas_call(functools.partial(low_rank_kernel, dp), out_shape=(jax.Sha...  2.45 us
    ppermute x1, starting transfers between devices, body(): other = lax.ppermute(partial, 'c', [(0, 1), (1, 0)])  1.92 us
  transfers between devices with their start and end apart: 1, of which 1 were waited for; matrix products, arithmetic and copies ran while one was open for 0% of the time, Pallas kernels for 0%

profile of v5, /device:TPU:2, one launch (start us, length us, event | category | flops | bytes accessed | tf_op | source)
XLA Modules:
  0.0 94.5 jit_solution(3527434642689484041)
XLA Ops:
  0.6 2.5 %low_rank.1 = (bf16[512,128]{1,0:T(8,128)(2,1)S(1)}, bf16[512,1024]{1,0:T(8,128)(2,1)S(1)}, bf16[512,1024]{1,0:T(8,128)(2,1)S(1)}, f32[1064,128]{1,0:T(8,128)S(1)}, f32[1056,128]{1,0:T(8,128)S(1)}) custom-call(bf16[512,1024]{1,0:T(8,128)(2,1)} %act.1, bf16[512,1024]{1,0:T(8,128)(2,1)} %cot.1, f32[64,1024]{1,0:T(8,128)} %bitcast.2, f32[64,1024]{1,0:T(8,128)} %up.1, ...), custom_call_target="tpu_custom_call" | custom-call | tf_op jit(solution)/shard_map/low_rank/pallas_call | solution.py:214
  3.1 1.9 %collective-permute-start = (bf16[512,128]{1,0:T(8,128)(2,1)S(1)}, bf16[512,128]{1,0:T(8,128)(2,1)S(1)}, u32[]{:S(2)}, u32[]{:S(2)}) collective-permute-start(bf16[512,128]{1,0:T(8,128)(2,1)S(1)} %get-tuple-element.12.mine), channel_id=1, source_target_pairs={{0,1},{1,0},{2,3},{3,2},{4,5},{5,4},{6,7},{7,6},{8,9},{9,8},{10,11... | collective-permute-start | bytes 393224 | tf_op jit(solution)/shard_map/ppermute | solution.py:236
  5.0 1.3 %collective-permute-done.other = bf16[512,128]{1,0:T(8,128)(2,1)S(1)} collective-permute-done((bf16[512,128]{1,0:T(8,128)(2,1)S(1)}, bf16[512,128]{1,0:T(8,128)(2,1)S(1)}, u32[]{:S(2)}, u32[]{:S(2)}) %collective-permute-start) | collective-permute-done | bytes 131104 | tf_op jit(solution)/shard_map/ppermute | solution.py:236
  6.4 20.6 %all_to_all.20.parts = bf16[4,512,128]{2,1,0:T(8,128)(2,1)S(1)} all-to-all(bf16[4,512,128]{2,1,0:T(8,128)(2,1)S(1)} %add_cores.1), channel_id=1, replica_groups=mesh['y'=8,'z'=12,'x'=4,'c'=2] {'x'}, dimensions={0} | all-to-all | bytes 1048576 | tf_op jit(solution)/shard_map/all_to_all | solution.py:245
  26.9 0.0 copy-start
  26.9 0.0 copy-start.1
  26.9 0.7 grads.1
  27.7 33.0 %all_to_all.21.parts = bf16[96,4,384]{2,1,0:T(4,128)(2,1)S(1)} all-to-all(bf16[96,4,384]{2,1,0:T(4,128)(2,1)S(1)} %grads.1), channel_id=1, replica_groups=mesh['y'=8,'z'=12,'x'=4,'c'=2] {'y','z'}, dimensions={0} | all-to-all | bytes 589824 | tf_op jit(solution)/shard_map/all_to_all | solution.py:258
  60.7 0.0 copy-done
  60.7 0.0 copy-done.1
  60.7 0.2 owner.1
  60.8 14.8 %all_to_all.22.source = bf16[12,2,1408]{2,1,0:T(2,128)(2,1)S(1)} all-to-all(bf16[12,2,1408]{2,1,0:T(2,128)(2,1)S(1)} %get-tuple-element.17), channel_id=1, replica_groups=mesh['y'=8,'z'=12,'x'=4,'c'=2] {'z'}, dimensions={0} | all-to-all | bytes 135168 | tf_op jit(solution)/shard_map/all_to_all | solution.py:274
  75.6 0.1 row_copies.1
  75.6 17.5 %all_to_all.23.moments = bf16[8,24,1408]{2,1,0:T(8,128)(2,1)S(1)} all-to-all(bf16[8,24,1408]{2,1,0:T(8,128)(2,1)S(1)} %row_copies.1), channel_id=1, replica_groups=mesh['y'=8,'z'=12,'x'=4,'c'=2] {'y'}, dimensions={0} | all-to-all | bytes 1081344 | tf_op jit(solution)/shard_map/all_to_all | solution.py:284
  93.2 1.3 %written.1 = (f32[3,1,1408]{2,1,0:T(1,128)}, f32[3,1056,128]{2,1,0:T(8,128)}) custom-call(f32[12,128]{1,0:T(8,128)S(1)} %get-tuple-element.15.own_one, f32[12,128]{1,0:T(8,128)S(1)} %get-tuple-element.16.own_two, bf16[8,24,1408]{2,1,0:T(8,128)(2,1)S(1)} %all_to_all.23.moments, f32[1064,128]{1,0:T(8,128)S(1)} %get-tuple-element.18.flat, ...), custom_call_target="tpu_custom_call" | custom-call | tf_op jit(solution)/shard_map/written/pallas_call | solution.py:285
  (1 shorter events, 0.0 us)
Async XLA Ops:
  3.1 3.2 %collective-permute-start = (bf16[512,128]{1,0:T(8,128)(2,1)S(1)}, bf16[512,128]{1,0:T(8,128)(2,1)S(1)}, u32[]{:S(2)}, u32[]{:S(2)}) collective-permute-start(bf16[512,128]{1,0:T(8,128)(2,1)S(1)} %get-tuple-element.12.mine), channel_id=1, source_target_pairs={{0,1},{1,0},{2,3},{3,2},{4,5},{5,4},{6,7},{7,6},{8,9},{9,8},{10,11... | collective-permute-start | bytes 393224 | tf_op jit(solution)/shard_map/ppermute | solution.py:236
  26.9 33.7 %copy-start = (f32[1,1408]{1,0:T(1,128)S(1)}, f32[1,1408]{1,0:T(1,128)}, u32[]{:S(2)}) copy-start(f32[1,1408]{1,0:T(1,128)} %first.1) | copy-start | bytes 16900
  26.9 33.7 %copy-start.1 = (f32[1,1408]{1,0:T(1,128)S(1)}, f32[1,1408]{1,0:T(1,128)}, u32[]{:S(2)}) copy-start(f32[1,1408]{1,0:T(1,128)} %second.1) | copy-start | bytes 16900

commit v6 on v5

--- a/solution.py
+++ b/solution.py
@@ -112,11 +112,20 @@
     up = 2.0 * jnp.dot(turned[:rank], cot[...], preferred_element_type=F32)
     down = 2.0 * jnp.dot(twice, act[...], preferred_element_type=F32)
     store_flat(flat, wide, down, up)
+    for j in range(out.shape[0]):
+        out[j] = flat[rows * j : rows * j + out.shape[1], :].astype(BF16)
+
+
+def slab_kernel(rows, parts, out, slab):
+    total = parts[0].astype(F32)
+    for j in range(1, parts.shape[0]):
+        total += parts[j].astype(F32)
+    slab[...] = total
     part = out.shape[1]
     for j in range(out.shape[0]):
         for i in range(out.shape[2] // LANES):
             at = rows * j + part * i
-            out[j, :, i * LANES : (i + 1) * LANES] = flat[at : at + part, :].astype(BF16)
+            out[j, :, i * LANES : (i + 1) * LANES] = slab[at : at + part, :].astype(BF16)
 
 
 def adam_moments(grad, moment_one, moment_two):
@@ -243,9 +252,12 @@
         name="add_cores",
     )(partial, other)
     parts = lax.all_to_all(copies, "x", 0, 0)
-    chunks = pl.pallas_call(
-        functools.partial(grad_kernel, rows),
-        out_shape=jax.ShapeDtypeStruct((dp_count, part, lanes), BF16),
+    y_count, z_count = lax.axis_size(dp[0]), lax.axis_size(dp[1])
+    slab = rows * z_count
+    tall = -(-slab // 8) * 8
+    slabs = pl.pallas_call(
+        functools.partial(grad_kernel, slab),
+        out_shape=jax.ShapeDtypeStruct((y_count, tall, LANES), BF16),
         in_specs=[VMEM] * 3,
         out_specs=VMEM,
         scratch_shapes=[
@@ -255,9 +267,18 @@
         compiler_params=PARAMS,
         name="grads",
     )(parts, act_copy, cot_copy)
-    mine = lax.all_to_all(chunks, dp, 0, 0)
+    column = lax.all_to_all(slabs, dp[0], 0, 0)
+    chunks = pl.pallas_call(
+        functools.partial(slab_kernel, rows),
+        out_shape=jax.ShapeDtypeStruct((z_count, part, lanes), BF16),
+        in_specs=[VMEM],
+        out_specs=VMEM,
+        scratch_shapes=[pltpu.VMEM((tall, LANES), F32)],
+        compiler_params=PARAMS,
+        name="slab",
+    )(column)
+    mine = lax.all_to_all(chunks, dp[1], 0, 0)
     half = lanes * part // LANES
-    z_count = lax.axis_size(dp[1])
     own_one, own_two, send = pl.pallas_call(
         functools.partial(owner_kernel, rows),
         out_shape=(

time: 94.8 us -> 95 us (level)
    all_to_all x1 -> x2, blocking collectives: 33 us -> 35.9 us  [the longest x1 21.5 us: body(): mine = lax.all_to_all(chunks, dp[1], 0, 0)]
    all_to_all x1, blocking collectives: 17.5 us -> 15.9 us  [body(): moments = lax.all_to_all(row_copies, dp[0], 0, 0)]
    all_to_all x1, blocking collectives: 14.8 us -> 13.6 us  [body(): row = lax.all_to_all(send, dp[1], 0, 0)]
where the time goes in v6:
time: 95 us; the launch traced here: 94.7 us
  blocking collectives  85.8 us (90%)
  Pallas kernels  4.99 us (5%)
  starting transfers between devices  1.92 us (2%)
  waiting for transfers between devices  1.31 us (1%)
    all_to_all x1, blocking collectives, body(): mine = lax.all_to_all(chunks, dp[1], 0, 0)  21.5 us
    all_to_all x1, blocking collectives, body(): parts = lax.all_to_all(copies, 'x', 0, 0)  20.4 us
    all_to_all x1, blocking collectives, body(): moments = lax.all_to_all(row_copies, dp[0], 0, 0)  15.9 us
    all_to_all x1, blocking collectives, body(): column = lax.all_to_all(slabs, dp[0], 0, 0)  14.4 us
    all_to_all x1, blocking collectives, body(): row = lax.all_to_all(send, dp[1], 0, 0)  13.6 us
    pallas_call x1, Pallas kernels, body(): pl.pallas_call(functools.partial(low_rank_kernel, dp), out_shape=(jax.Sha...  2.72 us
    ppermute x1, starting transfers between devices, body(): other = lax.ppermute(partial, 'c', [(0, 1), (1, 0)])  1.92 us
  transfers between devices with their start and end apart: 1, of which 1 were waited for; matrix products, arithmetic and copies ran while one was open for 0% of the time, Pallas kernels for 0%

profile of v6, /device:TPU:2, one launch (start us, length us, event | category | flops | bytes accessed | tf_op | source)
XLA Modules:
  0.0 94.7 jit_solution(9553951412877003840)
XLA Ops:
  0.6 2.7 %low_rank.1 = (bf16[512,128]{1,0:T(8,128)(2,1)S(1)}, bf16[512,1024]{1,0:T(8,128)(2,1)S(1)}, bf16[512,1024]{1,0:T(8,128)(2,1)S(1)}, f32[1064,128]{1,0:T(8,128)S(1)}, f32[1056,128]{1,0:T(8,128)S(1)}) custom-call(bf16[512,1024]{1,0:T(8,128)(2,1)} %act.1, bf16[512,1024]{1,0:T(8,128)(2,1)} %cot.1, f32[64,1024]{1,0:T(8,128)} %bitcast.2, f32[64,1024]{1,0:T(8,128)} %up.1, ...), custom_call_target="tpu_custom_call" | custom-call | tf_op jit(solution)/shard_map/low_rank/pallas_call | solution.py:223
  3.4 1.9 %collective-permute-start = (bf16[512,128]{1,0:T(8,128)(2,1)S(1)}, bf16[512,128]{1,0:T(8,128)(2,1)S(1)}, u32[]{:S(2)}, u32[]{:S(2)}) collective-permute-start(bf16[512,128]{1,0:T(8,128)(2,1)S(1)} %get-tuple-element.12.mine), channel_id=1, source_target_pairs={{0,1},{1,0},{2,3},{3,2},{4,5},{5,4},{6,7},{7,6},{8,9},{9,8},{10,11... | collective-permute-start | bytes 393224 | tf_op jit(solution)/shard_map/ppermute | solution.py:245
  5.3 1.3 %collective-permute-done.other = bf16[512,128]{1,0:T(8,128)(2,1)S(1)} collective-permute-done((bf16[512,128]{1,0:T(8,128)(2,1)S(1)}, bf16[512,128]{1,0:T(8,128)(2,1)S(1)}, u32[]{:S(2)}, u32[]{:S(2)}) %collective-permute-start) | collective-permute-done | bytes 131104 | tf_op jit(solution)/shard_map/ppermute | solution.py:245
  6.6 20.4 %all_to_all.25.parts = bf16[4,512,128]{2,1,0:T(8,128)(2,1)S(1)} all-to-all(bf16[4,512,128]{2,1,0:T(8,128)(2,1)S(1)} %add_cores.1), channel_id=1, replica_groups=mesh['y'=8,'z'=12,'x'=4,'c'=2] {'x'}, dimensions={0} | all-to-all | bytes 1048576 | tf_op jit(solution)/shard_map/all_to_all | solution.py:254
  27.1 0.0 copy-start
  27.1 0.0 copy-start.1
  27.1 0.7 grads.1
  27.8 14.4 %all_to_all.26.parts = bf16[8,136,128]{2,1,0:T(8,128)(2,1)S(1)} all-to-all(bf16[8,136,128]{2,1,0:T(8,128)(2,1)S(1)} %grads.1), channel_id=1, replica_groups=mesh['y'=8,'z'=12,'x'=4,'c'=2] {'y'}, dimensions={0} | all-to-all | bytes 557056 | tf_op jit(solution)/shard_map/all_to_all | solution.py:270
  42.2 0.1 slab.1
  42.3 21.5 %all_to_all.27.parts = bf16[12,4,384]{2,1,0:T(4,128)(2,1)S(1)} all-to-all(bf16[12,4,384]{2,1,0:T(4,128)(2,1)S(1)} %slab.1), channel_id=1, replica_groups=mesh['y'=8,'z'=12,'x'=4,'c'=2] {'z'}, dimensions={0} | all-to-all | bytes 73728 | tf_op jit(solution)/shard_map/all_to_all | solution.py:280
  63.7 0.0 copy-done
  63.7 0.0 copy-done.1
  63.7 0.1 owner.1
  63.8 13.6 %all_to_all.28.source = bf16[12,2,1408]{2,1,0:T(2,128)(2,1)S(1)} all-to-all(bf16[12,2,1408]{2,1,0:T(2,128)(2,1)S(1)} %get-tuple-element.17), channel_id=1, replica_groups=mesh['y'=8,'z'=12,'x'=4,'c'=2] {'z'}, dimensions={0} | all-to-all | bytes 135168 | tf_op jit(solution)/shard_map/all_to_all | solution.py:295
  77.4 0.1 row_copies.1
  77.5 15.9 %all_to_all.29.moments = bf16[8,24,1408]{2,1,0:T(8,128)(2,1)S(1)} all-to-all(bf16[8,24,1408]{2,1,0:T(8,128)(2,1)S(1)} %row_copies.1), channel_id=1, replica_groups=mesh['y'=8,'z'=12,'x'=4,'c'=2] {'y'}, dimensions={0} | all-to-all | bytes 1081344 | tf_op jit(solution)/shard_map/all_to_all | solution.py:305
  93.4 1.3 %written.1 = (f32[3,1,1408]{2,1,0:T(1,128)}, f32[3,1056,128]{2,1,0:T(8,128)}) custom-call(f32[12,128]{1,0:T(8,128)S(1)} %get-tuple-element.15.own_one, f32[12,128]{1,0:T(8,128)S(1)} %get-tuple-element.16.own_two, bf16[8,24,1408]{2,1,0:T(8,128)(2,1)S(1)} %all_to_all.29.moments, f32[1064,128]{1,0:T(8,128)S(1)} %get-tuple-element.18.flat, ...), custom_call_target="tpu_custom_call" | custom-call | tf_op jit(solution)/shard_map/written/pallas_call | solution.py:306
  (1 shorter events, 0.0 us)
Async XLA Ops:
  3.4 3.2 %collective-permute-start = (bf16[512,128]{1,0:T(8,128)(2,1)S(1)}, bf16[512,128]{1,0:T(8,128)(2,1)S(1)}, u32[]{:S(2)}, u32[]{:S(2)}) collective-permute-start(bf16[512,128]{1,0:T(8,128)(2,1)S(1)} %get-tuple-element.12.mine), channel_id=1, source_target_pairs={{0,1},{1,0},{2,3},{3,2},{4,5},{5,4},{6,7},{7,6},{8,9},{9,8},{10,11... | collective-permute-start | bytes 393224 | tf_op jit(solution)/shard_map/ppermute | solution.py:245
  27.1 36.7 %copy-start = (f32[1,1408]{1,0:T(1,128)S(1)}, f32[1,1408]{1,0:T(1,128)}, u32[]{:S(2)}) copy-start(f32[1,1408]{1,0:T(1,128)} %first.1) | copy-start | bytes 16900
  27.1 36.7 %copy-start.1 = (f32[1,1408]{1,0:T(1,128)S(1)}, f32[1,1408]{1,0:T(1,128)}, u32[]{:S(2)}) copy-start(f32[1,1408]{1,0:T(1,128)} %second.1) | copy-start | bytes 16900

commit v7 on v6

--- a/solution.py
+++ b/solution.py
@@ -116,16 +116,24 @@
         out[j] = flat[rows * j : rows * j + out.shape[1], :].astype(BF16)
 
 
-def slab_kernel(rows, parts, out, slab):
+def store_rows(target, start, source, rows):
+    for r in range(rows):
+        target[start + r : start + r + 1, :] = source[:, r * LANES : (r + 1) * LANES]
+
+
+def slab_kernel(rows, parts, first, second, out, both):
+    tall = parts.shape[1]
+    half = (out.shape[1] - tall) // 2
     total = parts[0].astype(F32)
     for j in range(1, parts.shape[0]):
         total += parts[j].astype(F32)
-    slab[...] = total
-    part = out.shape[1]
+    both[:tall, :] = total
+    both[tall:, :] = jnp.zeros((2 * half, LANES), F32)
+    store_rows(both, tall, first, rows)
+    store_rows(both, tall + half, second, rows)
+    values = both[...].astype(BF16)
     for j in range(out.shape[0]):
-        for i in range(out.shape[2] // LANES):
-            at = rows * j + part * i
-            out[j, :, i * LANES : (i + 1) * LANES] = slab[at : at + part, :].astype(BF16)
+        out[j] = values
 
 
 def adam_moments(grad, moment_one, moment_two):
@@ -138,47 +146,36 @@
     return param - 0.01 * (fresh_one / fixed_one) / (jnp.sqrt(fresh_two / fixed_two) + 1e-08)
 
 
-def own_moments(rows, first, second, one, two):
-    for r in range(rows):
-        one[r : r + 1, :] = first[:, r * LANES : (r + 1) * LANES]
-        two[r : r + 1, :] = second[:, r * LANES : (r + 1) * LANES]
-    blank = jnp.zeros((one.shape[0] - rows, LANES), F32)
-    one[rows:, :] = blank
-    two[rows:, :] = blank
-
-
-def owner_kernel(rows, parts, first, second, fresh_one, fresh_two, send, grad, one, two, both):
-    total = jnp.sum(parts[...].astype(F32), axis=0)
-    part = total.shape[0]
-    for i in range(total.shape[1] // LANES):
-        grad[part * i : part * (i + 1), :] = total[:, i * LANES : (i + 1) * LANES]
-    own_moments(rows, first, second, one, two)
-    fresh = adam_moments(grad[...], one[...], two[...])
-    fresh_one[...], fresh_two[...] = fresh
+def owner_kernel(rows, axis, parts, first, second, own_one, own_two, send, grad, one, two, mine_one, mine_two, both):
+    tall = grad.shape[0]
+    half = (parts.shape[1] - tall) // 2
+    slab = rows * parts.shape[0]
+    total = jnp.zeros((tall, LANES), F32)
+    for j in range(parts.shape[0]):
+        values = parts[j].astype(F32)
+        total += values[:tall]
+        one[rows * j : rows * j + half, :] = values[tall : tall + half]
+        two[rows * j : rows * j + half, :] = values[tall + half :]
+    grad[...] = total
+    fresh = adam_moments(total[:slab], one[:slab, :], two[:slab, :])
     for i in range(2):
-        for r in range(rows):
-            both[i : i + 1, r * LANES : (r + 1) * LANES] = fresh[i][r : r + 1, :]
+        both[slab * i : slab * (i + 1), :] = fresh[i]
     packed = both[...].astype(BF16)
     for j in range(send.shape[0]):
         send[j] = packed
-
-
-def row_kernel(source, out, wide):
-    count = source.shape[0]
-    for z in range(count):
-        pair = source[z].astype(F32)
-        for i in range(2):
-            wide[i * count + z : i * count + z + 1, :] = pair[i : i + 1]
-    values = wide[...].astype(BF16)
-    for y in range(out.shape[0]):
-        out[y] = values
+    blank = jnp.zeros((half - rows, LANES), F32)
+    for target, source in ((mine_one, first), (mine_two, second)):
+        store_rows(target, 0, source, rows)
+        target[rows:, :] = blank
+    mine = grad[pl.ds(lax.axis_index(axis) * rows, half), :]
+    own_one[...], own_two[...] = adam_moments(mine, mine_one[...], mine_two[...])
 
 
 def written_kernel(rows, dp, own_one, own_two, moments, flat, mask, own, out, one, two, fresh, mine, sems):
-    count = moments.shape[1] // 2
+    slab = moments.shape[1] // 2
     steps = sems.shape[0] - 1
     per_step = moments.shape[0] // steps
-    tall = per_step * count * rows
+    tall = per_step * slab
     values = own_one[...], own_two[...]
     values = (adam_param(flat[pl.ds(lax.axis_index(dp) * rows, own_one.shape[0]), :], *values),) + values
     for i in range(3):
@@ -188,11 +185,9 @@
     copies[0].start()
     for s in range(steps):
         for y in range(s * per_step, (s + 1) * per_step):
-            for r in range(rows):
-                values = moments[y, :, r * LANES : (r + 1) * LANES].astype(F32)
-                at = pl.ds(y * count * rows + r, count, stride=rows)
-                one[at, :] = values[:count]
-                two[at, :] = values[count:]
+            values = moments[y].astype(F32)
+            one[slab * y : slab * (y + 1), :] = values[:slab]
+            two[slab * y : slab * (y + 1), :] = values[slab:]
         for r in range(s * tall, (s + 1) * tall, 24):
             at = slice(r, r + 24)
             keep = mask[at, :] > 0.0
@@ -212,8 +207,6 @@
     part_len = first_moment.shape[1]
     rows = part_len // LANES
     all_rows = rows * dp_count
-    part = 4
-    lanes = -(-rows // part) * LANES
     tokens, width = activations.shape
     rank = factor_up.shape[0]
     down_t = factor_down.T
@@ -268,41 +261,33 @@
         name="grads",
     )(parts, act_copy, cot_copy)
     column = lax.all_to_all(slabs, dp[0], 0, 0)
-    chunks = pl.pallas_call(
+    half = -(-rows // 4) * 4
+    line = pl.pallas_call(
         functools.partial(slab_kernel, rows),
-        out_shape=jax.ShapeDtypeStruct((z_count, part, lanes), BF16),
-        in_specs=[VMEM],
+        out_shape=jax.ShapeDtypeStruct((z_count, tall + 2 * half, LANES), BF16),
+        in_specs=[VMEM] * 3,
         out_specs=VMEM,
-        scratch_shapes=[pltpu.VMEM((tall, LANES), F32)],
+        scratch_shapes=[pltpu.VMEM((tall + 2 * half, LANES), F32)],
         compiler_params=PARAMS,
         name="slab",
-    )(column)
-    mine = lax.all_to_all(chunks, dp[1], 0, 0)
-    half = lanes * part // LANES
+    )(column, first_moment, second_moment)
+    line = lax.all_to_all(line, dp[1], 0, 0)
     own_one, own_two, send = pl.pallas_call(
-        functools.partial(owner_kernel, rows),
+        functools.partial(owner_kernel, rows, dp[1]),
         out_shape=(
             jax.ShapeDtypeStruct((half, LANES), F32),
             jax.ShapeDtypeStruct((half, LANES), F32),
-            jax.ShapeDtypeStruct((z_count, 2, part_len), BF16),
+            jax.ShapeDtypeStruct((y_count, 2 * slab, LANES), BF16),
         ),
         in_specs=[VMEM] * 3,
         out_specs=(VMEM, VMEM, VMEM),
-        scratch_shapes=[pltpu.VMEM((half, LANES), F32)] * 3 + [pltpu.VMEM((2, part_len), F32)],
+        scratch_shapes=[pltpu.VMEM((tall, LANES), F32)] * 3
+        + [pltpu.VMEM((half, LANES), F32)] * 2
+        + [pltpu.VMEM((2 * slab, LANES), F32)],
         compiler_params=PARAMS,
         name="owner",
-    )(mine, first_moment, second_moment)
-    row = lax.all_to_all(send, dp[1], 0, 0)
-    row_copies = pl.pallas_call(
-        row_kernel,
-        out_shape=jax.ShapeDtypeStruct((lax.axis_size(dp[0]), 2 * z_count, part_len), BF16),
-        in_specs=[VMEM],
-        out_specs=VMEM,
-        scratch_shapes=[pltpu.VMEM((2 * z_count, part_len), F32)],
-        compiler_params=PARAMS,
-        name="row_copies",
-    )(row)
-    moments = lax.all_to_all(row_copies, dp[0], 0, 0)
+    )(line, first_moment, second_moment)
+    moments = lax.all_to_all(send, dp[0], 0, 0)
     partition, written = pl.pallas_call(
         functools.partial(written_kernel, rows, dp),
         out_shape=(

time: 95 us -> 96.1 us (1.012)
  the two profiles are of different devices: /device:TPU:2 before, /device:TPU:64 now
where the time goes in v7:
time: 96.1 us; the launch traced here: 95.8 us
  blocking collectives  87.1 us (91%)
  Pallas kernels  4.72 us (5%)
  starting transfers between devices  1.92 us (2%)
  waiting for transfers between devices  1.31 us (1%)
    all_to_all x1, blocking collectives, body(): line = lax.all_to_all(line, dp[1], 0, 0)  34.4 us
    all_to_all x1, blocking collectives, body(): moments = lax.all_to_all(send, dp[0], 0, 0)  20.9 us
    all_to_all x1, blocking collectives, body(): column = lax.all_to_all(slabs, dp[0], 0, 0)  18 us
    all_to_all x1, blocking collectives, body(): parts = lax.all_to_all(copies, 'x', 0, 0)  13.9 us
    pallas_call x1, Pallas kernels, body(): pl.pallas_call(functools.partial(low_rank_kernel, dp), out_shape=(jax.Sha...  2.46 us
  transfers between devices with their start and end apart: 1, of which 1 were waited for; matrix products, arithmetic and copies ran while one was open for 0% of the time, Pallas kernels for 0%

profile of v7, /device:TPU:64, one launch (start us, length us, event | category | flops | bytes accessed | tf_op | source)
XLA Modules:
  0.0 95.8 jit_solution(11357126314906676083)
XLA Ops:
  0.6 2.5 %low_rank.1 = (bf16[512,128]{1,0:T(8,128)(2,1)S(1)}, bf16[512,1024]{1,0:T(8,128)(2,1)S(1)}, bf16[512,1024]{1,0:T(8,128)(2,1)S(1)}, f32[1064,128]{1,0:T(8,128)S(1)}, f32[1056,128]{1,0:T(8,128)S(1)}) custom-call(bf16[512,1024]{1,0:T(8,128)(2,1)} %act.1, bf16[512,1024]{1,0:T(8,128)(2,1)} %cot.1, f32[64,1024]{1,0:T(8,128)} %bitcast.2, f32[64,1024]{1,0:T(8,128)} %up.1, ...), custom_call_target="tpu_custom_call" | custom-call | tf_op jit(solution)/shard_map/low_rank/pallas_call | solution.py:216
  3.1 1.9 %collective-permute-start = (bf16[512,128]{1,0:T(8,128)(2,1)S(1)}, bf16[512,128]{1,0:T(8,128)(2,1)S(1)}, u32[]{:S(2)}, u32[]{:S(2)}) collective-permute-start(bf16[512,128]{1,0:T(8,128)(2,1)S(1)} %get-tuple-element.12.mine), channel_id=1, source_target_pairs={{0,1},{1,0},{2,3},{3,2},{4,5},{5,4},{6,7},{7,6},{8,9},{9,8},{10,11... | collective-permute-start | bytes 393224 | tf_op jit(solution)/shard_map/ppermute | solution.py:238
  5.0 1.3 %collective-permute-done.other = bf16[512,128]{1,0:T(8,128)(2,1)S(1)} collective-permute-done((bf16[512,128]{1,0:T(8,128)(2,1)S(1)}, bf16[512,128]{1,0:T(8,128)(2,1)S(1)}, u32[]{:S(2)}, u32[]{:S(2)}) %collective-permute-start) | collective-permute-done | bytes 131104 | tf_op jit(solution)/shard_map/ppermute | solution.py:238
  6.4 13.9 %all_to_all.20.parts = bf16[4,512,128]{2,1,0:T(8,128)(2,1)S(1)} all-to-all(bf16[4,512,128]{2,1,0:T(8,128)(2,1)S(1)} %add_cores.1), channel_id=1, replica_groups=mesh['y'=8,'z'=12,'x'=4,'c'=2] {'x'}, dimensions={0} | all-to-all | bytes 1048576 | tf_op jit(solution)/shard_map/all_to_all | solution.py:247
  20.3 0.0 copy-start
  20.3 0.0 copy-start.1
  20.3 0.7 grads.1
  21.0 18.0 %all_to_all.21.parts = bf16[8,136,128]{2,1,0:T(8,128)(2,1)S(1)} all-to-all(bf16[8,136,128]{2,1,0:T(8,128)(2,1)S(1)} %grads.1), channel_id=1, replica_groups=mesh['y'=8,'z'=12,'x'=4,'c'=2] {'y'}, dimensions={0} | all-to-all | bytes 557056 | tf_op jit(solution)/shard_map/all_to_all | solution.py:263
  39.0 0.0 copy-done
  39.0 0.0 copy-done.1
  39.0 0.1 slab.1
  39.1 34.4 %all_to_all.22.parts = bf16[12,160,128]{2,1,0:T(8,128)(2,1)S(1)} all-to-all(bf16[12,160,128]{2,1,0:T(8,128)(2,1)S(1)} %slab.1), channel_id=1, replica_groups=mesh['y'=8,'z'=12,'x'=4,'c'=2] {'z'}, dimensions={0} | all-to-all | bytes 983040 | tf_op jit(solution)/shard_map/all_to_all | solution.py:274
  73.4 0.1 owner.1
  73.6 20.9 %all_to_all.23.moments = bf16[8,264,128]{2,1,0:T(8,128)(2,1)S(1)} all-to-all(bf16[8,264,128]{2,1,0:T(8,128)(2,1)S(1)} %get-tuple-element.17), channel_id=1, replica_groups=mesh['y'=8,'z'=12,'x'=4,'c'=2] {'y'}, dimensions={0} | all-to-all | bytes 1081344 | tf_op jit(solution)/shard_map/all_to_all | solution.py:290
  94.4 1.3 %written.1 = (f32[3,1,1408]{2,1,0:T(1,128)}, f32[3,1056,128]{2,1,0:T(8,128)}) custom-call(f32[12,128]{1,0:T(8,128)S(1)} %get-tuple-element.15.own_one, f32[12,128]{1,0:T(8,128)S(1)} %get-tuple-element.16.own_two, bf16[8,264,128]{2,1,0:T(8,128)(2,1)S(1)} %all_to_all.23.moments, f32[1064,128]{1,0:T(8,128)S(1)} %get-tuple-element.18.flat, ...), custom_call_target="tpu_custom_call" | custom-call | tf_op jit(solution)/shard_map/written/pallas_call | solution.py:291
  (1 shorter events, 0.0 us)
Async XLA Ops:
  3.1 3.2 %collective-permute-start = (bf16[512,128]{1,0:T(8,128)(2,1)S(1)}, bf16[512,128]{1,0:T(8,128)(2,1)S(1)}, u32[]{:S(2)}, u32[]{:S(2)}) collective-permute-start(bf16[512,128]{1,0:T(8,128)(2,1)S(1)} %get-tuple-element.12.mine), channel_id=1, source_target_pairs={{0,1},{1,0},{2,3},{3,2},{4,5},{5,4},{6,7},{7,6},{8,9},{9,8},{10,11... | collective-permute-start | bytes 393224 | tf_op jit(solution)/shard_map/ppermute | solution.py:238
  20.3 18.7 %copy-start = (f32[1,1408]{1,0:T(1,128)S(1)}, f32[1,1408]{1,0:T(1,128)}, u32[]{:S(2)}) copy-start(f32[1,1408]{1,0:T(1,128)} %first.3) | copy-start | bytes 16900
  20.3 18.7 %copy-start.1 = (f32[1,1408]{1,0:T(1,128)S(1)}, f32[1,1408]{1,0:T(1,128)}, u32[]{:S(2)}) copy-start(f32[1,1408]{1,0:T(1,128)} %second.3) | copy-start | bytes 16900

commit v8 on v5

--- a/solution.py
+++ b/solution.py
@@ -96,15 +96,21 @@
 
 
 def add_copies_kernel(mine, other, out):
-    total = (mine[...].astype(F32) + other[...].astype(F32)).astype(BF16)
-    for i in range(out.shape[0]):
-        out[i] = total
+    total = mine[...].astype(F32) + other[...].astype(F32)
+    tall = out.shape[1]
+    for k in range(out.shape[2] // LANES):
+        block = total[k * tall : (k + 1) * tall].astype(BF16)
+        for i in range(out.shape[0]):
+            out[i, :, k * LANES : (k + 1) * LANES] = block
 
 
 def grad_kernel(rows, parts, act, cot, out, flat, wide):
-    total = parts[0].astype(F32)
+    wide_total = parts[0].astype(F32)
     for i in range(1, parts.shape[0]):
-        total += parts[i].astype(F32)
+        wide_total += parts[i].astype(F32)
+    total = jnp.concatenate(
+        [wide_total[:, k * LANES : (k + 1) * LANES] for k in range(parts.shape[2] // LANES)], axis=0
+    )
     turned = total.T.astype(BF16)
     rank = turned.shape[0] // 2
     projected = turned[rank:]
@@ -236,7 +242,7 @@
     other = lax.ppermute(partial, "c", [(0, 1), (1, 0)])
     copies = pl.pallas_call(
         add_copies_kernel,
-        out_shape=jax.ShapeDtypeStruct((x_count, tokens, 2 * rank), BF16),
+        out_shape=jax.ShapeDtypeStruct((x_count, 16, tokens // 16 * 2 * rank), BF16),
         in_specs=[VMEM] * 2,
         out_specs=VMEM,
         compiler_params=PARAMS,

time: 94.8 us -> 94.9 us (level)
  no operation moved by 1% of the time
where the time goes in v8:
time: 94.9 us; the launch traced here: 94.5 us
  blocking collectives  85.8 us (90%)
  Pallas kernels  4.84 us (5%)
  starting transfers between devices  1.92 us (2%)
  waiting for transfers between devices  1.31 us (1%)
    all_to_all x1, blocking collectives, body(): mine = lax.all_to_all(chunks, dp, 0, 0)  33 us
    all_to_all x1, blocking collectives, body(): parts = lax.all_to_all(copies, 'x', 0, 0)  20.6 us
    all_to_all x1, blocking collectives, body(): moments = lax.all_to_all(row_copies, dp[0], 0, 0)  17.5 us
    all_to_all x1, blocking collectives, body(): row = lax.all_to_all(send, dp[1], 0, 0)  14.8 us
    pallas_call x1, Pallas kernels, body(): pl.pallas_call(functools.partial(low_rank_kernel, dp), out_shape=(jax.Sha...  2.45 us
    ppermute x1, starting transfers between devices, body(): other = lax.ppermute(partial, 'c', [(0, 1), (1, 0)])  1.92 us
  transfers between devices with their start and end apart: 1, of which 1 were waited for; matrix products, arithmetic and copies ran while one was open for 0% of the time, Pallas kernels for 0%

profile of v8, /device:TPU:2, one launch (start us, length us, event | category | flops | bytes accessed | tf_op | source)
XLA Modules:
  0.0 94.5 jit_solution(17327335063634077339)
XLA Ops:
  0.6 2.5 %low_rank.1 = (bf16[512,128]{1,0:T(8,128)(2,1)S(1)}, bf16[512,1024]{1,0:T(8,128)(2,1)S(1)}, bf16[512,1024]{1,0:T(8,128)(2,1)S(1)}, f32[1064,128]{1,0:T(8,128)S(1)}, f32[1056,128]{1,0:T(8,128)S(1)}) custom-call(bf16[512,1024]{1,0:T(8,128)(2,1)} %act.1, bf16[512,1024]{1,0:T(8,128)(2,1)} %cot.1, f32[64,1024]{1,0:T(8,128)} %bitcast.2, f32[64,1024]{1,0:T(8,128)} %up.1, ...), custom_call_target="tpu_custom_call" | custom-call | tf_op jit(solution)/shard_map/low_rank/pallas_call | solution.py:220
  3.1 1.9 %collective-permute-start = (bf16[512,128]{1,0:T(8,128)(2,1)S(1)}, bf16[512,128]{1,0:T(8,128)(2,1)S(1)}, u32[]{:S(2)}, u32[]{:S(2)}) collective-permute-start(bf16[512,128]{1,0:T(8,128)(2,1)S(1)} %get-tuple-element.12.mine), channel_id=1, source_target_pairs={{0,1},{1,0},{2,3},{3,2},{4,5},{5,4},{6,7},{7,6},{8,9},{9,8},{10,11... | collective-permute-start | bytes 393224 | tf_op jit(solution)/shard_map/ppermute | solution.py:242
  5.0 1.3 %collective-permute-done.other = bf16[512,128]{1,0:T(8,128)(2,1)S(1)} collective-permute-done((bf16[512,128]{1,0:T(8,128)(2,1)S(1)}, bf16[512,128]{1,0:T(8,128)(2,1)S(1)}, u32[]{:S(2)}, u32[]{:S(2)}) %collective-permute-start) | collective-permute-done | bytes 131104 | tf_op jit(solution)/shard_map/ppermute | solution.py:242
  6.3 0.1 add_cores.1
  6.4 20.6 %all_to_all.20.parts = bf16[4,16,4096]{2,1,0:T(8,128)(2,1)S(1)} all-to-all(bf16[4,16,4096]{2,1,0:T(8,128)(2,1)S(1)} %add_cores.1), channel_id=1, replica_groups=mesh['y'=8,'z'=12,'x'=4,'c'=2] {'x'}, dimensions={0} | all-to-all | bytes 1048576 | tf_op jit(solution)/shard_map/all_to_all | solution.py:251
  27.0 0.0 copy-start
  27.0 0.0 copy-start.1
  27.0 0.7 grads.1
  27.7 33.0 %all_to_all.21.parts = bf16[96,4,384]{2,1,0:T(4,128)(2,1)S(1)} all-to-all(bf16[96,4,384]{2,1,0:T(4,128)(2,1)S(1)} %grads.1), channel_id=1, replica_groups=mesh['y'=8,'z'=12,'x'=4,'c'=2] {'y','z'}, dimensions={0} | all-to-all | bytes 589824 | tf_op jit(solution)/shard_map/all_to_all | solution.py:264
  60.7 0.0 copy-done
  60.7 0.0 copy-done.1
  60.7 0.2 owner.1
  60.9 14.8 %all_to_all.22.source = bf16[12,2,1408]{2,1,0:T(2,128)(2,1)S(1)} all-to-all(bf16[12,2,1408]{2,1,0:T(2,128)(2,1)S(1)} %get-tuple-element.17), channel_id=1, replica_groups=mesh['y'=8,'z'=12,'x'=4,'c'=2] {'z'}, dimensions={0} | all-to-all | bytes 135168 | tf_op jit(solution)/shard_map/all_to_all | solution.py:280
  75.6 0.1 row_copies.1
  75.7 17.5 %all_to_all.23.moments = bf16[8,24,1408]{2,1,0:T(8,128)(2,1)S(1)} all-to-all(bf16[8,24,1408]{2,1,0:T(8,128)(2,1)S(1)} %row_copies.1), channel_id=1, replica_groups=mesh['y'=8,'z'=12,'x'=4,'c'=2] {'y'}, dimensions={0} | all-to-all | bytes 1081344 | tf_op jit(solution)/shard_map/all_to_all | solution.py:290
  93.2 1.3 %written.1 = (f32[3,1,1408]{2,1,0:T(1,128)}, f32[3,1056,128]{2,1,0:T(8,128)}) custom-call(f32[12,128]{1,0:T(8,128)S(1)} %get-tuple-element.15.own_one, f32[12,128]{1,0:T(8,128)S(1)} %get-tuple-element.16.own_two, bf16[8,24,1408]{2,1,0:T(8,128)(2,1)S(1)} %all_to_all.23.moments, f32[1064,128]{1,0:T(8,128)S(1)} %get-tuple-element.18.flat, ...), custom_call_target="tpu_custom_call" | custom-call | tf_op jit(solution)/shard_map/written/pallas_call | solution.py:291
Async XLA Ops:
  3.1 3.2 %collective-permute-start = (bf16[512,128]{1,0:T(8,128)(2,1)S(1)}, bf16[512,128]{1,0:T(8,128)(2,1)S(1)}, u32[]{:S(2)}, u32[]{:S(2)}) collective-permute-start(bf16[512,128]{1,0:T(8,128)(2,1)S(1)} %get-tuple-element.12.mine), channel_id=1, source_target_pairs={{0,1},{1,0},{2,3},{3,2},{4,5},{5,4},{6,7},{7,6},{8,9},{9,8},{10,11... | collective-permute-start | bytes 393224 | tf_op jit(solution)/shard_map/ppermute | solution.py:242
  27.0 33.7 %copy-start = (f32[1,1408]{1,0:T(1,128)S(1)}, f32[1,1408]{1,0:T(1,128)}, u32[]{:S(2)}) copy-start(f32[1,1408]{1,0:T(1,128)} %first.1) | copy-start | bytes 16900
  27.0 33.7 %copy-start.1 = (f32[1,1408]{1,0:T(1,128)S(1)}, f32[1,1408]{1,0:T(1,128)}, u32[]{:S(2)}) copy-start(f32[1,1408]{1,0:T(1,128)} %second.1) | copy-start | bytes 16900
